TPU v7x, 128 devices: a whole 4x4x4 slice. The times are simulated.
128 devices in a mesh: gx: 8 (over z_hi, y), gy: 16 (over x, z_lo, core).
Axes of the slice: x: 4, y: 4, z: 4 (z_hi: 2, z_lo: 2; z = z_hi * 2 + z_lo), core: 2. Of those that a mesh axis runs over, the one named last changes fastest.
Arguments:
- wave_now: float32 [3, 32, 256, 2048], P(None, None, 'gx', 'gy'), may hold values from -5 to 5, as said below
- wave_prev: float32 [3, 32, 256, 2048], P(None, None, 'gx', 'gy'), may hold values from -6 to 6
- shear_mod: float32 [32, 256, 2048], P(None, 'gx', 'gy'), may hold values from 0.02 to 0.06
- bulk_mod: float32 [32, 256, 2048], P(None, 'gx', 'gy'), may hold values from 0.02 to 0.08
- found_cell: int32 [8, 16, 128, 4], P('gx', 'gy'), may hold values from 0 to 4095
- support_row: int32 [2, 16384], P(None, ('gx', 'gy')), may hold values from 0 to 511, as said below
- block_col: int32 [16, 4, 16384], P(None, None, ('gx', 'gy')), may hold values from 0 to 15, as said below
- block_val: float32 [16, 4, 6, 6, 16384], P(None, None, None, None, ('gx', 'gy')), may hold values from -0.36 to 0.36
- mass_inv: float32 [16, 6, 16384], P(None, None, ('gx', 'gy')), may hold values from 0.5 to 1.5
- bridge_disp: float32 [16, 6, 16384], P(None, None, ('gx', 'gy')), may hold values from -6 to 6
- bridge_vel: float32 [16, 6, 16384], P(None, None, ('gx', 'gy')), may hold values from -6 to 6
- bridge_acc: float32 [16, 6, 16384], P(None, None, ('gx', 'gy')), may hold values from -6 to 6
Outputs:
- wave_out: float32 [3, 32, 256, 2048], P(None, None, 'gx', 'gy')
- wave_before: float32 [3, 32, 256, 2048], P(None, None, 'gx', 'gy')
- deck_disp: float32 [16, 6, 16384], P(None, None, ('gx', 'gy'))
- deck_vel: float32 [16, 6, 16384], P(None, None, ('gx', 'gy'))
Inputs may be any that keep to these rules, and one draw needn't show every extreme that they name: `wave_now`: normal values clipped to the range; in other draws a broad positive part may be added. `support_row`: for each owner, the 2 x 128 entries of its bridge sections are distinct and fill all 4 slots of exactly 64 source tiles; which tiles varies by owner. `block_col`: in each block row of each section the 4 block columns are distinct and the first is the row itself.
All inputs are finite; a program needn't handle non-finite values.
Results may differ from a plain program's by a relative error of at most 0.0001.
Values sent between devices are 32-bit elements; how exact they have to be, the bound alone decides.
A program may use at most 64 MiB of HBM per device.

v0:
```python
import jax
import jax.numpy as jnp
from jax import lax
from jax.sharding import PartitionSpec as P

STEPS = 10


def with_halo(cells, sides, width):
    for axis, dim in sides:
        count = lax.axis_size(axis)
        ends = count - 1
        head = lax.slice_in_dim(cells, 0, width, axis=dim)
        tail = lax.slice_in_dim(cells, cells.shape[dim] - width, cells.shape[dim], axis=dim)
        cells = jnp.concatenate(
            [
                lax.ppermute(tail, axis, [(i, (i + 1) % count) for i in range(ends)]),
                cells,
                lax.ppermute(head, axis, [((i + 1) % count, i) for i in range(ends)]),
            ],
            axis=dim,
        )
    return cells


def first_diff(padded, which_axis):
    length = padded.shape[which_axis] - 4
    pieces = [
        lax.slice_in_dim(padded, offset, offset + length, axis=which_axis) for offset in range(5)
    ]
    return (pieces[0] - 8.0 * pieces[1] + 8.0 * pieces[3] - pieces[4]) / 12.0


def second_diff(padded, which_axis):
    length = padded.shape[which_axis] - 4
    pieces = [
        lax.slice_in_dim(padded, offset, offset + length, axis=which_axis) for offset in range(5)
    ]
    return (-pieces[0] + 16.0 * pieces[1] - 30.0 * pieces[2] + 16.0 * pieces[3] - pieces[4]) / 12.0


def interior(values, keep_axes, inner_shape):
    for which_axis in range(3):
        if which_axis not in keep_axes:
            values = lax.slice_in_dim(values, 2, 2 + inner_shape[which_axis], axis=which_axis)
    return values


def wave_accel(padded, shear_mod, bulk_mod):
    inner_shape = shear_mod.shape
    axis_of = (1, 2, 0)
    result = []
    for component in range(3):
        field = padded[component]
        own_axis = axis_of[component]
        curves = [
            second_diff(interior(field, (which_axis,), inner_shape), which_axis)
            for which_axis in range(3)
        ]
        laplace = curves[0] + curves[1] + curves[2]
        diverge = curves[own_axis]
        for second in range(3):
            if second != component:
                other_axis = axis_of[second]
                block = interior(padded[second], (own_axis, other_axis), inner_shape)
                diverge = diverge + first_diff(first_diff(block, other_axis), own_axis)
        result.append(shear_mod * laplace + bulk_mod * diverge)
    return result


def wave_substep(current, previous, shear_mod, bulk_mod):
    extended = with_halo(current, (("gx", 2), ("gy", 3)), 2)
    padded = jnp.pad(extended, ((0, 0), (2, 2), (0, 0), (0, 0)))
    accel = wave_accel(padded, shear_mod, bulk_mod)
    return jnp.stack(
        [
            2.0 * current[component] - previous[component] + accel[component]
            for component in range(3)
        ]
    )


def surface_rows(current, slot_cells):
    surface = current[:, 0].reshape(current.shape[0], -1)
    return surface[:, slot_cells]


def pick_ground(received, support_row):
    flat_rows = received.reshape(received.shape[0], -1)
    return flat_rows[:, support_row]


def stiff_apply(displace, block_val, block_col):
    node_count = displace.shape[0]
    onehot = (
        block_col[:, :, None, :] == jnp.arange(node_count, dtype=jnp.int32)[None, None, :, None]
    ).astype(jnp.float32)
    picked = jnp.sum(onehot[:, :, :, None, :] * displace[None, None, :, :, :], axis=2)
    return displace + jnp.sum(block_val * picked[:, :, None, :, :], axis=(1, 3))


def bridge_advance(displace, velocity, accelerate, ground, mass_inv, block_val, block_col):
    new_disp = displace + velocity + 0.5 * accelerate
    node_count = displace.shape[0]
    forcing = jnp.zeros_like(displace)
    forcing = forcing.at[0, 0:3].set(ground[:, 0])
    forcing = forcing.at[node_count - 1, 0:3].set(ground[:, 1])
    new_acc = mass_inv * (forcing - stiff_apply(new_disp, block_val, block_col))
    new_vel = velocity + 0.5 * (accelerate + new_acc)
    return (new_disp, new_vel, new_acc)


def local(
    wave_now,
    wave_prev,
    shear_mod,
    bulk_mod,
    found_cell,
    support_row,
    block_col,
    block_val,
    mass_inv,
    bridge_disp,
    bridge_vel,
    bridge_acc,
):
    slot_cells = found_cell[0, 0]
    start_state = (wave_now, wave_prev, bridge_disp, bridge_vel, bridge_acc)

    def advance_one(counter, state_now):
        current, previous, displace, velocity, accelerate = state_now
        following = wave_substep(current, previous, shear_mod, bulk_mod)
        outgoing = surface_rows(following, slot_cells)
        received = lax.all_to_all(outgoing, ("gx", "gy"), split_axis=1, concat_axis=1, tiled=True)
        ground = pick_ground(received, support_row)
        displace, velocity, accelerate = bridge_advance(
            displace, velocity, accelerate, ground, mass_inv, block_val, block_col
        )
        return (following, current, displace, velocity, accelerate)

    final_state = lax.fori_loop(0, STEPS, advance_one, start_state)
    current, previous, displace, velocity, accelerate = final_state
    return (current, previous, displace, velocity)


def solution(mesh):
    in_specs = (
        P(None, None, "gx", "gy"),
        P(None, None, "gx", "gy"),
        P(None, "gx", "gy"),
        P(None, "gx", "gy"),
        P("gx", "gy", None, None),
        P(None, ("gx", "gy")),
        P(None, None, ("gx", "gy")),
        P(None, None, None, None, ("gx", "gy")),
        P(None, None, ("gx", "gy")),
        P(None, None, ("gx", "gy")),
        P(None, None, ("gx", "gy")),
        P(None, None, ("gx", "gy")),
    )
    out_specs = (
        P(None, None, "gx", "gy"),
        P(None, None, "gx", "gy"),
        P(None, None, ("gx", "gy")),
        P(None, None, ("gx", "gy")),
    )
    return jax.shard_map(local, mesh=mesh, in_specs=in_specs, out_specs=out_specs, check_vma=False)
```

profile of v0, /device:TPU:1, one launch (start us, length us, event | category | flops | bytes accessed | tf_op | source)
XLA Modules:
  0.0 895.0 jit_solution(16176899737379254521)
XLA Ops:
  4.2 889.5 %while.23 = (s32[]{:T(128)}, f32[3,32,32,128]{3,2,1,0:T(8,128)S(1)}, f32[3,32,32,128]{3,2,1,0:T(8,128)}, f32[16,6,128]{2,1,0:T(8,128)S(1)}, f32[16,6,128]{2,1,0:...) while((s32[]{:T(128)}, ...), condition=%wide.region_3.0_spmd, body=%wide.region_0.3_spmd.sunk | while | flops 29878528 | bytes 108357448 | solution.py:141
  43.3 8.4 fusion.124
  70.2 15.1 %all-to-all-start = ((f32[3,128,4]{0,2,1:T(4,128)}), f32[3,128,4]{0,2,1:T(4,128)S(1)}, u32[]{:S(2)}, u32[]{:S(2)}) async-start(f32[3,128,4]{0,2,1:T(4,128)} %bitcast.74), calls=%async_computation | async-start | bytes 524288 | tf_op jit(solution)/shard_map/while/body/eval_jaxpr/all_to_all | solution.py:134
  85.3 11.0 %all-to-all-done = f32[3,128,4]{0,2,1:T(4,128)S(1)} async-done(((f32[3,128,4]{0,2,1:T(4,128)}), f32[3,128,4]{0,2,1:T(4,128)S(1)}, u32[]{:S(2)}, u32[]{:S(2)}) %all-to-all-start) | async-done | bytes 6176 | tf_op jit(solution)/shard_map/while/body/eval_jaxpr/all_to_all | solution.py:134
  161.2 12.6 %all-to-all-start = ((f32[3,128,4]{0,2,1:T(4,128)}), f32[3,128,4]{0,2,1:T(4,128)S(1)}, u32[]{:S(2)}, u32[]{:S(2)}) async-start(f32[3,128,4]{0,2,1:T(4,128)} %bitcast.74), calls=%async_computation | async-start | bytes 524288 | tf_op jit(solution)/shard_map/while/body/eval_jaxpr/all_to_all | solution.py:134
  173.8 11.0 %all-to-all-done = f32[3,128,4]{0,2,1:T(4,128)S(1)} async-done(((f32[3,128,4]{0,2,1:T(4,128)}), f32[3,128,4]{0,2,1:T(4,128)S(1)}, u32[]{:S(2)}, u32[]{:S(2)}) %all-to-all-start) | async-done | bytes 6176 | tf_op jit(solution)/shard_map/while/body/eval_jaxpr/all_to_all | solution.py:134
  249.7 12.6 %all-to-all-start = ((f32[3,128,4]{0,2,1:T(4,128)}), f32[3,128,4]{0,2,1:T(4,128)S(1)}, u32[]{:S(2)}, u32[]{:S(2)}) async-start(f32[3,128,4]{0,2,1:T(4,128)} %bitcast.74), calls=%async_computation | async-start | bytes 524288 | tf_op jit(solution)/shard_map/while/body/eval_jaxpr/all_to_all | solution.py:134
  262.3 11.0 %all-to-all-done = f32[3,128,4]{0,2,1:T(4,128)S(1)} async-done(((f32[3,128,4]{0,2,1:T(4,128)}), f32[3,128,4]{0,2,1:T(4,128)S(1)}, u32[]{:S(2)}, u32[]{:S(2)}) %all-to-all-start) | async-done | bytes 6176 | tf_op jit(solution)/shard_map/while/body/eval_jaxpr/all_to_all | solution.py:134
  338.2 12.6 %all-to-all-start = ((f32[3,128,4]{0,2,1:T(4,128)}), f32[3,128,4]{0,2,1:T(4,128)S(1)}, u32[]{:S(2)}, u32[]{:S(2)}) async-start(f32[3,128,4]{0,2,1:T(4,128)} %bitcast.74), calls=%async_computation | async-start | bytes 524288 | tf_op jit(solution)/shard_map/while/body/eval_jaxpr/all_to_all | solution.py:134
  350.8 11.0 %all-to-all-done = f32[3,128,4]{0,2,1:T(4,128)S(1)} async-done(((f32[3,128,4]{0,2,1:T(4,128)}), f32[3,128,4]{0,2,1:T(4,128)S(1)}, u32[]{:S(2)}, u32[]{:S(2)}) %all-to-all-start) | async-done | bytes 6176 | tf_op jit(solution)/shard_map/while/body/eval_jaxpr/all_to_all | solution.py:134
  399.7 8.4 fusion.124
  426.6 12.6 %all-to-all-start = ((f32[3,128,4]{0,2,1:T(4,128)}), f32[3,128,4]{0,2,1:T(4,128)S(1)}, u32[]{:S(2)}, u32[]{:S(2)}) async-start(f32[3,128,4]{0,2,1:T(4,128)} %bitcast.74), calls=%async_computation | async-start | bytes 524288 | tf_op jit(solution)/shard_map/while/body/eval_jaxpr/all_to_all | solution.py:134
  439.3 11.0 %all-to-all-done = f32[3,128,4]{0,2,1:T(4,128)S(1)} async-done(((f32[3,128,4]{0,2,1:T(4,128)}), f32[3,128,4]{0,2,1:T(4,128)S(1)}, u32[]{:S(2)}, u32[]{:S(2)}) %all-to-all-start) | async-done | bytes 6176 | tf_op jit(solution)/shard_map/while/body/eval_jaxpr/all_to_all | solution.py:134
  488.2 8.4 fusion.124
  515.1 12.6 %all-to-all-start = ((f32[3,128,4]{0,2,1:T(4,128)}), f32[3,128,4]{0,2,1:T(4,128)S(1)}, u32[]{:S(2)}, u32[]{:S(2)}) async-start(f32[3,128,4]{0,2,1:T(4,128)} %bitcast.74), calls=%async_computation | async-start | bytes 524288 | tf_op jit(solution)/shard_map/while/body/eval_jaxpr/all_to_all | solution.py:134
  527.7 11.0 %all-to-all-done = f32[3,128,4]{0,2,1:T(4,128)S(1)} async-done(((f32[3,128,4]{0,2,1:T(4,128)}), f32[3,128,4]{0,2,1:T(4,128)S(1)}, u32[]{:S(2)}, u32[]{:S(2)}) %all-to-all-start) | async-done | bytes 6176 | tf_op jit(solution)/shard_map/while/body/eval_jaxpr/all_to_all | solution.py:134
  603.6 12.6 %all-to-all-start = ((f32[3,128,4]{0,2,1:T(4,128)}), f32[3,128,4]{0,2,1:T(4,128)S(1)}, u32[]{:S(2)}, u32[]{:S(2)}) async-start(f32[3,128,4]{0,2,1:T(4,128)} %bitcast.74), calls=%async_computation | async-start | bytes 524288 | tf_op jit(solution)/shard_map/while/body/eval_jaxpr/all_to_all | solution.py:134
  616.2 11.0 %all-to-all-done = f32[3,128,4]{0,2,1:T(4,128)S(1)} async-done(((f32[3,128,4]{0,2,1:T(4,128)}), f32[3,128,4]{0,2,1:T(4,128)S(1)}, u32[]{:S(2)}, u32[]{:S(2)}) %all-to-all-start) | async-done | bytes 6176 | tf_op jit(solution)/shard_map/while/body/eval_jaxpr/all_to_all | solution.py:134
  692.1 12.6 %all-to-all-start = ((f32[3,128,4]{0,2,1:T(4,128)}), f32[3,128,4]{0,2,1:T(4,128)S(1)}, u32[]{:S(2)}, u32[]{:S(2)}) async-start(f32[3,128,4]{0,2,1:T(4,128)} %bitcast.74), calls=%async_computation | async-start | bytes 524288 | tf_op jit(solution)/shard_map/while/body/eval_jaxpr/all_to_all | solution.py:134
  704.7 11.0 %all-to-all-done = f32[3,128,4]{0,2,1:T(4,128)S(1)} async-done(((f32[3,128,4]{0,2,1:T(4,128)}), f32[3,128,4]{0,2,1:T(4,128)S(1)}, u32[]{:S(2)}, u32[]{:S(2)}) %all-to-all-start) | async-done | bytes 6176 | tf_op jit(solution)/shard_map/while/body/eval_jaxpr/all_to_all | solution.py:134
  780.6 12.6 %all-to-all-start = ((f32[3,128,4]{0,2,1:T(4,128)}), f32[3,128,4]{0,2,1:T(4,128)S(1)}, u32[]{:S(2)}, u32[]{:S(2)}) async-start(f32[3,128,4]{0,2,1:T(4,128)} %bitcast.74), calls=%async_computation | async-start | bytes 524288 | tf_op jit(solution)/shard_map/while/body/eval_jaxpr/all_to_all | solution.py:134
  793.2 11.0 %all-to-all-done = f32[3,128,4]{0,2,1:T(4,128)S(1)} async-done(((f32[3,128,4]{0,2,1:T(4,128)}), f32[3,128,4]{0,2,1:T(4,128)S(1)}, u32[]{:S(2)}, u32[]{:S(2)}) %all-to-all-start) | async-done | bytes 6176 | tf_op jit(solution)/shard_map/while/body/eval_jaxpr/all_to_all | solution.py:134
  869.1 12.6 %all-to-all-start = ((f32[3,128,4]{0,2,1:T(4,128)}), f32[3,128,4]{0,2,1:T(4,128)S(1)}, u32[]{:S(2)}, u32[]{:S(2)}) async-start(f32[3,128,4]{0,2,1:T(4,128)} %bitcast.74), calls=%async_computation | async-start | bytes 524288 | tf_op jit(solution)/shard_map/while/body/eval_jaxpr/all_to_all | solution.py:134
  881.7 11.0 %all-to-all-done = f32[3,128,4]{0,2,1:T(4,128)S(1)} async-done(((f32[3,128,4]{0,2,1:T(4,128)}), f32[3,128,4]{0,2,1:T(4,128)S(1)}, u32[]{:S(2)}, u32[]{:S(2)}) %all-to-all-start) | async-done | bytes 6176 | tf_op jit(solution)/shard_map/while/body/eval_jaxpr/all_to_all | solution.py:134
  (645 shorter events, 628.1 us)
Async XLA Ops:
  4.2 7.8 collective-permute-start
  17.2 9.4 %collective-permute-start.2 = (f32[3,32,36,2]{2,1,3,0:T(8,128)S(1)}, f32[3,32,36,2]{2,1,3,0:T(8,128)S(1)}, u32[]{:S(2)}, u32[]{:S(2)}) collective-permute-start(f32[3,32,36,2]{2,1,3,0:T(8,128)S(1)} %copy.83), channel_id=1, source_target_pairs={{1,0},{2,1},{3,2},{4,3},{5,4},{6,5},{7,6},{8,7},{9,8},{10,9},{11,1... | collective-permute-start | bytes 82952 | tf_op jit(solution)/shard_map/while/body/eval_jaxpr/ppermute | solution.py:19
  70.2 26.1 %all-to-all-start = ((f32[3,128,4]{0,2,1:T(4,128)}), f32[3,128,4]{0,2,1:T(4,128)S(1)}, u32[]{:S(2)}, u32[]{:S(2)}) async-start(f32[3,128,4]{0,2,1:T(4,128)} %bitcast.74), calls=%async_computation | async-start | bytes 524288 | tf_op jit(solution)/shard_map/while/body/eval_jaxpr/all_to_all | solution.py:134
  97.4 7.1 collective-permute-start
  109.7 7.9 collective-permute-start.2
  161.2 23.6 %all-to-all-start = ((f32[3,128,4]{0,2,1:T(4,128)}), f32[3,128,4]{0,2,1:T(4,128)S(1)}, u32[]{:S(2)}, u32[]{:S(2)}) async-start(f32[3,128,4]{0,2,1:T(4,128)} %bitcast.74), calls=%async_computation | async-start | bytes 524288 | tf_op jit(solution)/shard_map/while/body/eval_jaxpr/all_to_all | solution.py:134
  185.9 7.1 collective-permute-start
  198.2 7.9 collective-permute-start.2
  249.7 23.6 %all-to-all-start = ((f32[3,128,4]{0,2,1:T(4,128)}), f32[3,128,4]{0,2,1:T(4,128)S(1)}, u32[]{:S(2)}, u32[]{:S(2)}) async-start(f32[3,128,4]{0,2,1:T(4,128)} %bitcast.74), calls=%async_computation | async-start | bytes 524288 | tf_op jit(solution)/shard_map/while/body/eval_jaxpr/all_to_all | solution.py:134
  274.4 7.1 collective-permute-start
  286.6 7.9 collective-permute-start.2
  338.2 23.6 %all-to-all-start = ((f32[3,128,4]{0,2,1:T(4,128)}), f32[3,128,4]{0,2,1:T(4,128)S(1)}, u32[]{:S(2)}, u32[]{:S(2)}) async-start(f32[3,128,4]{0,2,1:T(4,128)} %bitcast.74), calls=%async_computation | async-start | bytes 524288 | tf_op jit(solution)/shard_map/while/body/eval_jaxpr/all_to_all | solution.py:134
  375.1 7.9 collective-permute-start.2
  426.6 23.6 %all-to-all-start = ((f32[3,128,4]{0,2,1:T(4,128)}), f32[3,128,4]{0,2,1:T(4,128)S(1)}, u32[]{:S(2)}, u32[]{:S(2)}) async-start(f32[3,128,4]{0,2,1:T(4,128)} %bitcast.74), calls=%async_computation | async-start | bytes 524288 | tf_op jit(solution)/shard_map/while/body/eval_jaxpr/all_to_all | solution.py:134
  463.6 7.9 collective-permute-start.2
  515.1 23.6 %all-to-all-start = ((f32[3,128,4]{0,2,1:T(4,128)}), f32[3,128,4]{0,2,1:T(4,128)S(1)}, u32[]{:S(2)}, u32[]{:S(2)}) async-start(f32[3,128,4]{0,2,1:T(4,128)} %bitcast.74), calls=%async_computation | async-start | bytes 524288 | tf_op jit(solution)/shard_map/while/body/eval_jaxpr/all_to_all | solution.py:134
  552.1 7.9 collective-permute-start.2
  603.6 23.6 %all-to-all-start = ((f32[3,128,4]{0,2,1:T(4,128)}), f32[3,128,4]{0,2,1:T(4,128)S(1)}, u32[]{:S(2)}, u32[]{:S(2)}) async-start(f32[3,128,4]{0,2,1:T(4,128)} %bitcast.74), calls=%async_computation | async-start | bytes 524288 | tf_op jit(solution)/shard_map/while/body/eval_jaxpr/all_to_all | solution.py:134
  640.6 7.9 collective-permute-start.2
  692.1 23.6 %all-to-all-start = ((f32[3,128,4]{0,2,1:T(4,128)}), f32[3,128,4]{0,2,1:T(4,128)S(1)}, u32[]{:S(2)}, u32[]{:S(2)}) async-start(f32[3,128,4]{0,2,1:T(4,128)} %bitcast.74), calls=%async_computation | async-start | bytes 524288 | tf_op jit(solution)/shard_map/while/body/eval_jaxpr/all_to_all | solution.py:134
  729.1 7.9 collective-permute-start.2
  780.6 23.6 %all-to-all-start = ((f32[3,128,4]{0,2,1:T(4,128)}), f32[3,128,4]{0,2,1:T(4,128)S(1)}, u32[]{:S(2)}, u32[]{:S(2)}) async-start(f32[3,128,4]{0,2,1:T(4,128)} %bitcast.74), calls=%async_computation | async-start | bytes 524288 | tf_op jit(solution)/shard_map/while/body/eval_jaxpr/all_to_all | solution.py:134
  817.5 7.9 collective-permute-start.2
  869.1 23.6 %all-to-all-start = ((f32[3,128,4]{0,2,1:T(4,128)}), f32[3,128,4]{0,2,1:T(4,128)S(1)}, u32[]{:S(2)}, u32[]{:S(2)}) async-start(f32[3,128,4]{0,2,1:T(4,128)} %bitcast.74), calls=%async_computation | async-start | bytes 524288 | tf_op jit(solution)/shard_map/while/body/eval_jaxpr/all_to_all | solution.py:134
  (116 other events, 577.9 us)
where the time goes:
time: 899 us; the launch traced here: 895 us
  other arithmetic  322 us (36%)
  starting transfers between devices  239 us (27%)
  local copies, waits for them, and re-layouts  220 us (24%)
  waiting for transfers between devices  110 us (12%)
    another operation x40, other arithmetic, wave_substep(): jnp.stack([2.0 * current[component] - previous[component] + accel[compone...  199 us
    all_to_all x10, starting transfers between devices, advance_one(): lax.all_to_all(outgoing, ('gx', 'gy'), split_axis=1, concat_axis=1, tiled...  128 us
    all_to_all x10, waiting for transfers between devices, advance_one(): lax.all_to_all(outgoing, ('gx', 'gy'), split_axis=1, concat_axis=1, tiled...  110 us
    ppermute x20, starting transfers between devices, with_halo(): lax.ppermute(tail, axis, [(i, (i + 1) % count) for i in range(ends)])  65.3 us
    div x30, other arithmetic, first_diff(): return (pieces[0] - 8.0 * pieces[1] + 8.0 * pieces[3] - pieces[4]) / 12.0  63.1 us
    slice x30, local copies, waits for them, and re-layouts, with_halo(): lax.slice_in_dim(cells, cells.shape[dim] - width, cells.shape[dim], axis=...  48.7 us
    concatenate x20, other arithmetic, with_halo(): jnp.concatenate([lax.ppermute(tail, axis, [(i, (i + 1) % count) for i in...  45.2 us
    ppermute x20, starting transfers between devices, with_halo(): lax.ppermute(head, axis, [((i + 1) % count, i) for i in range(ends)])  45.2 us
  transfers between devices with their start and end apart: 50, of which 10 were waited for; matrix products, arithmetic and copies ran while one was open for 7% of the time, Pallas kernels for 0%

commit v1 on v0

v1 whole, which is shorter than its diff:
```python
import functools

import jax
import jax.numpy as jnp
import ml_dtypes
import numpy as np
from jax import lax
from jax.experimental import pallas as pl
from jax.experimental.pallas import tpu as pltpu
from jax.sharding import PartitionSpec as P

MESH = pl.DeviceIdType.MESH
F32, BF = jnp.float32, jnp.bfloat16
STEPS = 10
GX, GY = 8, 16
R = 144
GR = 4
VMEM = pltpu.VMEM


def band(coefs, delta):
    k, n = np.arange(128)[:, None], np.arange(128)[None, :]
    dx = (k // 32 + 4 * delta) - n // 32
    dz = k % 32 - n % 32
    out = np.zeros((128, 128), np.float32)
    for (a, b), v in coefs.items():
        out[(dx == a) & (dz == b)] = v
    return out


def band_weights():
    c1 = {-2: 1, -1: -8, 1: 8, 2: -1}
    c2 = {-2: -1, -1: 16, 0: -30, 1: 16, 2: -1}
    dx = {(a, 0): v for a, v in c1.items()}
    dz = {(0, a): v for a, v in c1.items()}
    dxx = {(a, 0): v for a, v in c2.items()}
    dzz = {(0, a): v for a, v in c2.items()}
    dxz = {(a, b): v * w for a, v in c1.items() for b, w in c1.items()}
    lap = dict(dxx)
    for key, v in dzz.items():
        lap[key] = lap.get(key, 0) + v
    dxx12 = {key: 12 * v for key, v in dxx.items()}
    dzz12 = {key: 12 * v for key, v in dzz.items()}

    def two(m):
        return np.concatenate([m, m], 0)

    def beside(o):
        return np.where(np.arange(128)[:, None] < 64, band(o, 1), band(o, -1))

    def inner(ops):
        return np.concatenate([two(band(o, 0)) for o in ops], 1)

    def full(ops):
        return np.concatenate([inner(ops), np.concatenate([two(beside(o)) for o in ops], 1)], 0)

    def select(c):
        k, n = np.arange(128)[:, None], np.arange(128)[None, :]
        return two(((k % 32 == 0) & (n % 12 == c * 4 + k // 32) & (n < 120)).astype(np.float32))

    wu = full([lap, dxx12, dxz, dx])
    ww = full([lap, dxz])
    ww0 = inner([dzz12, dz])
    wv = full([lap, dx])
    wv0 = np.concatenate([inner([dz]), select(1)], 1)
    wsel = np.stack([select(0), select(2)])
    return [jnp.asarray(a.astype(ml_dtypes.bfloat16)) for a in (wu, ww, ww0, wv, wv0, wsel)]


def d1(m2, m1, p1, p2):
    return (m2 - p2) + 8.0 * (p1 - m1)


def wave_kernel(
    now, prev, shear, bulk, found, wu, ww, ww0, wv, wv0, wsel,
    out_now, out_prev, out_ground,
    WA, WB, SB, BH, MU, HU, HIST, PS, PR, send_sem, recv_sem,
):
    gx, gy = lax.axis_index("gx"), lax.axis_index("gy")

    def has(dx, dy):
        return (gx + dx >= 0) & (gx + dx < GX) & (gy + dy >= 0) & (gy + dy < GY)

    dirs = [(1, 0), (-1, 0), (0, 1), (0, -1), (1, 1), (1, -1), (-1, 1), (-1, -1)]
    WS = (WA, WB)
    lane = lax.broadcasted_iota(jnp.int32, (64, 128), 1)

    for W in WS:
        W[...] = jnp.zeros_like(W)
    PR[...] = jnp.zeros_like(PR)
    BH[...] = jnp.zeros_like(BH)
    HIST[...] = jnp.zeros_like(HIST)

    barrier = pltpu.get_barrier_semaphore()
    count = 0
    for dx, dy in dirs:
        ok = has(dx, dy)
        count = count + ok.astype(jnp.int32)

        @pl.when(ok)
        def _():
            pl.semaphore_signal(barrier, inc=1, device_id={"gx": gx + dx, "gy": gy + dy}, device_id_type=MESH)

    for c in range(3):
        for src, W in ((now, WA), (prev, WB)):

            def load_field(xs, _):
                rows = [src[c, pl.ds(xs * 4 + xl + 256 * q, 8, stride=32), :] for xl in range(4) for q in range(4)]
                W[c, xs + 1, 8:136, :] = jnp.concatenate(rows, 0).T
                return 0

            lax.fori_loop(0, 8, load_field, 0)
    for i, src in enumerate((shear, bulk)):

        def load_mod(xs, _):
            rows = [src[pl.ds(xs * 4 + xl + 256 * q, 8, stride=32), :] for xl in range(4) for q in range(4)]
            SB[i, xs] = jnp.concatenate(rows, 0).T * (1.0 / 12.0 if i == 0 else 1.0 / 144.0)
            return 0

        lax.fori_loop(0, 8, load_mod, 0)

    pl.semaphore_wait(barrier, count)

    def copy(p, d):
        dx, dy = dirs[d]
        W = WS[p]
        if dy == 0:
            side = 1 if dx > 0 else 0
            src, dst = PS.at[p, side], PR.at[p, 1 - side]
        else:
            y_src, y_dst = (134, 6) if dy > 0 else (8, 136)
            if dx == 0:
                src, dst = W.at[:, 1:9, pl.ds(y_src, 2), :], W.at[:, 1:9, pl.ds(y_dst, 2), :]
            else:
                x_src, x_dst = (8, 0) if dx > 0 else (1, 9)
                src, dst = W.at[0:2, x_src, pl.ds(y_src, 2), :], W.at[0:2, x_dst, pl.ds(y_dst, 2), :]
        return pltpu.make_async_remote_copy(
            src_ref=src, dst_ref=dst, send_sem=send_sem.at[p, d], recv_sem=recv_sem.at[p, d],
            device_id={"gx": gx + dx, "gy": gy + dy}, device_id_type=MESH,
        )

    def send(p):
        W = WS[p]
        for c in range(3):
            low, high = W[c, 8, 8:72, :], W[c, 8, 72:136, :]
            PS[p, 1, c] = jnp.where(lane < 64, pltpu.roll(low, 64, 1), high)
            low, high = W[c, 1, 8:72, :], W[c, 1, 72:136, :]
            PS[p, 0, c] = jnp.where(lane < 64, low, pltpu.roll(high, 64, 1))
        for d, (dx, dy) in enumerate(dirs):

            @pl.when(has(dx, dy))
            def _():
                copy(p, d).start()

    def finish(p):
        for d, (dx, dy) in enumerate(dirs):

            @pl.when(has(-dx, -dy))
            def _():
                copy(p, d).wait_recv()

        for d, (dx, dy) in enumerate(dirs):

            @pl.when(has(dx, dy))
            def _():
                copy(p, d).wait_send()

        W = WS[p]
        for c in range(3):
            left, right = PR[p, 0, c], PR[p, 1, c]
            W[c, 0, 8:72, :] = pltpu.roll(left, 64, 1)
            W[c, 0, 72:136, :] = left
            W[c, 9, 8:72, :] = right
            W[c, 9, 72:136, :] = pltpu.roll(right, 64, 1)

    def split_slab(W, c, xs, own=True, up=True, down=True):
        x = W[c, xs]
        hi = x.astype(BF)
        lo = (x - hi.astype(F32)).astype(BF)
        at = xs * R if isinstance(xs, int) else pl.multiple_of(xs * R, R)
        if own:
            BH[c, pl.ds(at, R), 0:128] = hi
            BH[c, pl.ds(at, R), 128:256] = lo
        if up:
            BH[c, pl.ds(at + R, R), 320:384] = hi[:, 64:128]
            BH[c, pl.ds(at + R, R), 448:512] = lo[:, 64:128]
        if down:
            BH[c, pl.ds(at - R, R), 256:320] = hi[:, 0:64]
            BH[c, pl.ds(at - R, R), 384:448] = lo[:, 0:64]

    def split_all(W):
        def body(xs, _):
            for c in range(3):
                split_slab(W, c, xs + 1)
            return 0

        lax.fori_loop(0, 8, body, 0)
        for c in range(3):
            split_slab(W, c, 0, own=False, down=False)
            split_slab(W, c, 9, own=False, up=False)

    dot = functools.partial(jnp.dot, preferred_element_type=F32)
    n = GR * R

    def matmuls(g):
        at = pl.multiple_of(g * n + R, R)
        u = dot(BH[0, pl.ds(at, n), :], wu[...])
        w = dot(BH[2, pl.ds(at, n), :], ww[...])
        w0 = dot(BH[2, pl.ds(at, n), 0:256], ww0[...])
        v = dot(BH[1, pl.ds(at, n), :], wv[...])
        v0 = dot(BH[1, pl.ds(at, n), 0:256], wv0[...])
        part = lambda a: a.reshape(GR, R, 128)
        MU[0] = part(u[:, 0:128])
        MU[1] = part(v[:, 0:128])
        MU[2] = part(w[:, 0:128])
        MU[3] = part(u[:, 128:256] + w[:, 128:256])
        MU[4] = part(u[:, 256:384] + w0[:, 0:128])
        MU[5] = part(u[:, 384:512] + w0[:, 128:256])
        MU[6] = part(v[:, 128:256])
        MU[7] = part(v0[:, 0:128])
        return v0[:, 128:256]

    def surface(g, picked, t):
        at = pl.multiple_of(g * n + R, R)
        picked = picked + dot(BH[0, pl.ds(at, n), 0:256], wsel[0]) + dot(BH[2, pl.ds(at, n), 0:256], wsel[1])
        group = lax.broadcasted_iota(jnp.int32, (GR, 128, 128), 2) // 12
        where = pl.ds(g * GR, GR)
        HIST[where] = jnp.where(group == t, picked.reshape(GR, R, 128)[:, 8:136, :], HIST[where])

    def update(g, j, W, N):
        xs = g * GR + j
        D = (-2, -1, 1, 2)
        for yb in range(16):
            r = lambda d: pl.ds(8 + yb * 8 + d, 8)
            sh = SB[0, xs, yb * 8 : yb * 8 + 8, :]
            bu = SB[1, xs, yb * 8 : yb * 8 + 8, :]
            mix = [
                MU[3, j, r(0), :] + d1(*[MU[6, j, r(d), :] for d in D]),
                d1(*[MU[5, j, r(d), :] for d in D]),
                MU[4, j, r(0), :] + d1(*[MU[7, j, r(d), :] for d in D]),
            ]
            for c in range(3):
                y = [W[c, xs + 1, r(d), :] for d in D]
                mid = W[c, xs + 1, r(0), :]
                dyy = 16.0 * (y[1] + y[2]) - (y[0] + y[3]) - 30.0 * mid
                lap = MU[c, j, r(0), :] + dyy
                b = mix[c] + 12.0 * dyy if c == 1 else mix[c]
                N[c, xs + 1, r(0), :] = (2.0 * mid - N[c, xs + 1, r(0), :]) + (sh * lap + bu * b)

    def substep(p, t):
        W, N = WS[p], WS[1 - p]
        finish(p)
        split_all(W)

        def body(g, _):
            picked = matmuls(g)
            surface(g, picked, t)
            for j in range(GR):
                update(g, j, W, N)
            return 0

        lax.fori_loop(0, 8 // GR, body, 0)

    send(0)

    def pair(i, _):
        substep(0, 2 * i - 1)
        send(1)
        substep(1, 2 * i)

        @pl.when(i < STEPS // 2 - 1)
        def _():
            send(0)

        return 0

    lax.fori_loop(0, STEPS // 2, pair, 0)

    def last(xs, _):
        for c in range(3):
            split_slab(WA, c, xs + 1, up=False, down=False)
        return 0

    lax.fori_loop(0, 8, last, 0)

    def last_surface(g, _):
        at = pl.multiple_of(g * n + R, R)
        surface(g, dot(BH[1, pl.ds(at, n), 0:256], wv0[:, 128:256]), STEPS - 1)
        return 0

    lax.fori_loop(0, 8 // GR, last_surface, 0)

    cell = found[...]
    row = (cell // 512) * 128 + cell % 128
    quarter = (cell // 128) % 4
    total = jnp.zeros((512, 256), F32)
    for i in range(4):
        pick = (row == lax.broadcasted_iota(jnp.int32, (512, 256), 1) + 256 * i).astype(F32).astype(BF)
        h = HIST[2 * i : 2 * i + 2].reshape(256, 128)
        hi = h.astype(BF)
        lo = (h - hi.astype(F32)).astype(BF)
        total = total + dot(pick, jnp.concatenate([hi, lo], 1))
    keep = lax.broadcasted_iota(jnp.int32, (512, 128), 1) % 4 == quarter
    out_ground[...] = jnp.where(keep, total[:, 0:128] + total[:, 128:256], 0.0)

    for c in range(3):
        for dst, W in ((out_now, WA), (out_prev, WB)):

            def store_field(xs, _):
                m = W[c, xs + 1, 8:136, :].T
                for xl in range(4):
                    for q in range(4):
                        dst[c, pl.ds(xs * 4 + xl + 256 * q, 8, stride=32), :] = m[(xl * 4 + q) * 8 : (xl * 4 + q) * 8 + 8]
                return 0

            lax.fori_loop(0, 8, store_field, 0)


def bridge_kernel(
    received, support, col, val_hbm, mass, disp, vel, acc,
    out_disp, out_vel,
    val, ground, state, sem,
):
    copies = []
    for node in range(16):
        c = pltpu.make_async_copy(val_hbm.at[node], val.at[:, :, :, node, :], sem.at[node])
        c.start()
        copies.append(c)
    rows = lax.broadcasted_iota(jnp.int32, (512, 128), 0)
    pick = jnp.concatenate([(rows == support[k : k + 1, :]).astype(F32).astype(BF) for k in range(2)], 1)
    flat = jnp.concatenate([received[128 * i : 128 * i + 128, :].T for i in range(4)], 1)
    hi = flat.astype(BF)
    lo = (flat - hi.astype(F32)).astype(BF)
    dot = functools.partial(jnp.dot, preferred_element_type=F32)
    ground[...] = jnp.sum((dot(hi, pick) + dot(lo, pick)).reshape(32, 4, 256), axis=1, keepdims=True)
    D, V, A = 0, 6, 12
    for d in range(6):
        state[D + d] = disp[:, d, :]
        state[V + d] = vel[:, d, :]
        state[A + d] = acc[:, d, :]
        state[18 + d] = mass[:, d, :]
    for c in copies:
        c.wait()
    sub = lax.broadcasted_iota(jnp.int32, (16, 128), 0)
    index = [col[:, j, :] for j in range(1, 4)]

    def step(t, _):
        new = [state[D + d] + state[V + d] + 0.5 * state[A + d] for d in range(6)]
        total = list(new)
        for j in range(4):
            for d in range(6):
                if j == 0:
                    v = new[d]
                else:
                    halves = []
                    for h in range(2):
                        ix = index[j - 1][8 * h : 8 * h + 8]
                        at = jnp.bitwise_and(ix, 7)
                        g0 = jnp.take_along_axis(new[d][0:8], at, axis=0)
                        g1 = jnp.take_along_axis(new[d][8:16], at, axis=0)
                        halves.append(jnp.where(ix >= 8, g1, g0))
                    v = jnp.concatenate(halves, 0)
                for e in range(6):
                    total[e] = total[e] + val[j, e, d] * v
        for d in range(6):
            force = -total[d]
            if d < 3:
                g = ground[t * 3 + d]
                force = force + jnp.where(sub == 0, g[:, 0:128], jnp.where(sub == 15, g[:, 128:256], 0.0))
            new_acc = state[18 + d] * force
            state[V + d] = state[V + d] + 0.5 * (state[A + d] + new_acc)
            state[A + d] = new_acc
            state[D + d] = new[d]
        return 0

    lax.fori_loop(0, STEPS, step, 0)
    for d in range(6):
        out_disp[:, d, :] = state[D + d]
        out_vel[:, d, :] = state[V + d]


def local(
    wave_now, wave_prev, shear_mod, bulk_mod, found_cell, support_row, block_col, block_val,
    mass_inv, bridge_disp, bridge_vel, bridge_acc,
):
    weights = band_weights()
    vm = pl.BlockSpec(memory_space=VMEM)
    now, before, outgoing = pl.pallas_call(
        wave_kernel,
        out_shape=[
            jax.ShapeDtypeStruct((3, 1024, 128), F32),
            jax.ShapeDtypeStruct((3, 1024, 128), F32),
            jax.ShapeDtypeStruct((512, 128), F32),
        ],
        in_specs=[vm] * 11,
        out_specs=[vm] * 3,
        scratch_shapes=[
            VMEM((3, 10, R, 128), F32),
            VMEM((3, 10, R, 128), F32),
            VMEM((2, 8, 128, 128), F32),
            VMEM((3, 10 * R, 512), BF),
            VMEM((8, GR, R, 128), F32),
            VMEM((8, 128), F32),
            VMEM((8, 128, 128), F32),
            VMEM((2, 2, 3, 64, 128), F32),
            VMEM((2, 2, 3, 64, 128), F32),
            pltpu.SemaphoreType.DMA((2, 8)),
            pltpu.SemaphoreType.DMA((2, 8)),
        ],
        compiler_params=pltpu.CompilerParams(
            collective_id=0, has_side_effects=True, vmem_limit_bytes=56 * 2**20
        ),
    )(
        wave_now.reshape(3, 1024, 128), wave_prev.reshape(3, 1024, 128),
        shear_mod.reshape(1024, 128), bulk_mod.reshape(1024, 128),
        found_cell.reshape(512, 1), *weights,
    )
    received = lax.all_to_all(
        outgoing.reshape(128, 4, 128), ("gx", "gy"), split_axis=0, concat_axis=0, tiled=True
    ).reshape(512, 128)
    deck_disp, deck_vel = pl.pallas_call(
        bridge_kernel,
        out_shape=[jax.ShapeDtypeStruct((16, 6, 128), F32)] * 2,
        in_specs=[vm] * 3 + [pl.BlockSpec(memory_space=pl.ANY)] + [vm] * 4,
        out_specs=[vm] * 2,
        scratch_shapes=[
            VMEM((4, 6, 6, 16, 128), F32),
            VMEM((32, 1, 256), F32),
            VMEM((24, 16, 128), F32),
            pltpu.SemaphoreType.DMA((16,)),
        ],
        compiler_params=pltpu.CompilerParams(vmem_limit_bytes=32 * 2**20),
    )(received, support_row, block_col, block_val, mass_inv, bridge_disp, bridge_vel, bridge_acc)
    return now.reshape(3, 32, 32, 128), before.reshape(3, 32, 32, 128), deck_disp, deck_vel


def solution(mesh):
    xy = ("gx", "gy")
    in_specs = (
        P(None, None, "gx", "gy"),
        P(None, None, "gx", "gy"),
        P(None, "gx", "gy"),
        P(None, "gx", "gy"),
        P("gx", "gy", None, None),
        P(None, xy),
        P(None, None, xy),
        P(None, None, None, None, xy),
        P(None, None, xy),
        P(None, None, xy),
        P(None, None, xy),
        P(None, None, xy),
    )
    out_specs = (
        P(None, None, "gx", "gy"),
        P(None, None, "gx", "gy"),
        P(None, None, xy),
        P(None, None, xy),
    )
    return jax.shard_map(local, mesh=mesh, in_specs=in_specs, out_specs=out_specs, check_vma=False)
```

time: 899 us -> 148 us (0.16)
  other arithmetic: 322 us -> 0 us
  starting transfers between devices: 239 us -> 11.2 us
  local copies, waits for them, and re-layouts: 220 us -> 6.77 us
  Pallas kernels: 0 us -> 119 us
  waiting for transfers between devices: 110 us -> 10.1 us
    another operation x40 -> x0, other arithmetic: 199 us -> none  [wave_substep(): jnp.stack([2.0 * current[component] - previous[component] + accel[compone...]
    pallas_call x0 -> x2, Pallas kernels: none -> 119 us  [the longest x1 116 us: local(): pl.pallas_call(wave_kernel, out_shape=[jax.ShapeDtypeStruct((3, 1024, 128...]
    all_to_all x10 -> x1, starting transfers between devices: 128 us -> 11.2 us  [local(): lax.all_to_all(outgoing.reshape(128, 4, 128), ('gx', 'gy'), split_axis=0,...]
    ppermute x40 -> x0, starting transfers between devices: 111 us -> none  [the longest x20 65.3 us: with_halo(): lax.ppermute(tail, axis, [(i, (i + 1) % count) for i in range(ends)])]
    slice x70 -> x0, local copies, waits for them, and re-layouts: 108 us -> none  [the longest x30 48.7 us: with_halo(): lax.slice_in_dim(cells, cells.shape[dim] - width, cells.shape[dim], axis=...]
    all_to_all x10 -> x1, waiting for transfers between devices: 110 us -> 10.1 us  [local(): lax.all_to_all(outgoing.reshape(128, 4, 128), ('gx', 'gy'), split_axis=0,...]
    div x30 -> x0, other arithmetic: 63.1 us -> none  [first_diff(): return (pieces[0] - 8.0 * pieces[1] + 8.0 * pieces[3] - pieces[4]) / 12.0]
    concatenate x20 -> x0, other arithmetic: 45.2 us -> none  [with_halo(): jnp.concatenate([lax.ppermute(tail, axis, [(i, (i + 1) % count) for i in...]
  transfers between devices with their start and end apart: 50 -> 1, of which waited for: 10 -> 1; matrix products, arithmetic and copies ran while one was open for 7% -> 0% of each run, Pallas kernels for 0% -> 0%
where the time goes in v1:
time: 148 us
  Pallas kernels  119 us (80%)
  starting transfers between devices  11.2 us (8%)
  waiting for transfers between devices  10.1 us (7%)
  local copies, waits for them, and re-layouts  6.77 us (5%)
    pallas_call x1, Pallas kernels, local(): pl.pallas_call(wave_kernel, out_shape=[jax.ShapeDtypeStruct((3, 1024, 128...  116 us
    all_to_all x1, starting transfers between devices, local(): lax.all_to_all(outgoing.reshape(128, 4, 128), ('gx', 'gy'), split_axis=0,...  11.2 us
    all_to_all x1, waiting for transfers between devices, local(): lax.all_to_all(outgoing.reshape(128, 4, 128), ('gx', 'gy'), split_axis=0,...  10.1 us
    unnamed x28, local copies, waits for them, and re-layouts  5.95 us
    pallas_call x1, Pallas kernels, local(): pl.pallas_call(bridge_kernel, out_shape=[jax.ShapeDtypeStruct((16, 6, 128...  3.39 us
  transfers between devices with their start and end apart: 1, of which 1 were waited for; matrix products, arithmetic and copies ran while one was open for 0% of the time, Pallas kernels for 0%

profile of v1, /device:TPU:1, one launch (start us, length us, event | category | flops | bytes accessed | tf_op | source)
XLA Modules:
  0.0 147.8 jit_solution(11108371108041701820)
XLA Ops:
  0.6 0.8 copy.30
  1.4 0.8 reshape.44.found
  2.2 115.5 %shard_map.201 = (f32[3,1024,128]{2,1,0:T(8,128)}, f32[3,1024,128]{2,1,0:T(8,128)}, f32[512,128]{1,0:T(8,128)}) custom-call(f32[3,1024,128]{2,1,0:T(8,128)} %bitcast.13, f32[3,1024,128]{2,1,0:T(8,128)} %bitcast.14, f32[1024,128]{1,0:T(8,128)} %bitcast.15, f32[1024,128]{1,0:T(8,128)} %bitcast.16, s32[512,1]{1,0:T(8,128)} %reshape.44.found, ...), custom_call_target="tpu_custom_call" | custom-call | tf_op jit(solution)/shard_map/pallas_call | solution.py:388
  117.8 0.0 copy-start.5
  117.8 0.0 copy-start.6
  117.8 11.2 %all-to-all-start = ((f32[128,4,128]{2,1,0:T(4,128)}), f32[128,4,128]{2,1,0:T(4,128)S(1)}, u32[]{:S(2)}, u32[]{:S(2)}) async-start(f32[128,4,128]{2,1,0:T(4,128)} %bitcast.17), calls=%async_computation | async-start | bytes 524288 | tf_op jit(solution)/shard_map/all_to_all | solution.py:418
  129.0 0.0 copy-start.7
  129.0 0.0 copy-start.8
  129.0 0.0 copy-done.4
  129.1 0.0 copy-start
  129.1 0.0 copy-start.1
  129.1 0.2 copy.32.val_hbm
  129.3 0.0 copy-done.5
  129.4 0.5 copy-done.7
  129.8 0.0 copy-done.8
  129.9 10.1 %all-to-all-done = f32[128,4,128]{2,1,0:T(4,128)S(1)} async-done(((f32[128,4,128]{2,1,0:T(4,128)}), f32[128,4,128]{2,1,0:T(4,128)S(1)}, u32[]{:S(2)}, u32[]{:S(2)}) %all-to-all-start) | async-done | bytes 262176 | tf_op jit(solution)/shard_map/all_to_all | solution.py:418
  140.0 0.0 copy-done.1
  140.0 3.4 %shard_map.202 = (f32[16,6,128]{2,1,0:T(8,128)S(1)}, f32[16,6,128]{2,1,0:T(8,128)S(1)}) custom-call(f32[512,128]{1,0:T(8,128)S(1)} %bitcast.10, s32[2,128]{1,0:T(2,128)S(1)} %copy-done.1, s32[16,4,128]{2,1,0:T(4,128)S(1)} %copy-done, f32[16,4,6,6,128]{4,3,2,1,0:T(8,128)S(1)} %copy.32.val_hbm, f32[16,6,128]{2,1,0:T(8,128)S(1)} %copy.33.mass, ...), custom_call_target="tpu_custom_call" | custom-call | tf_op jit(solution)/shard_map/pallas_call | solution.py:421
  143.4 0.6 copy.37
  144.0 0.6 copy.38
  144.7 0.0 copy-done.3
  144.7 1.1 copy.41
  145.8 0.8 copy-done.2
  146.6 1.1 copy.42
  (9 shorter events, 0.1 us)
Async XLA Ops:
  2.2 126.8 %copy-start.4 = (f32[16,4,6,6,128]{4,1,3,2,0:T(4,128)S(1)}, f32[16,4,6,6,128]{4,1,3,2,0:T(4,128)}, u32[]{:S(2)}) copy-start(f32[16,4,6,6,128]{4,1,3,2,0:T(4,128)} %param.25) | copy-start | bytes 3538948
  117.8 11.5 %copy-start.5 = (f32[16,6,128]{2,0,1:T(8,128)S(1)}, f32[16,6,128]{2,0,1:T(8,128)}, u32[]{:S(2)}) copy-start(f32[16,6,128]{2,0,1:T(8,128)} %param.26) | copy-start | bytes 147460
  117.8 11.5 %copy-start.6 = (f32[16,6,128]{2,0,1:T(8,128)S(1)}, f32[16,6,128]{2,0,1:T(8,128)}, u32[]{:S(2)}) copy-start(f32[16,6,128]{2,0,1:T(8,128)} %param.27) | copy-start | bytes 147460
  117.8 22.2 %all-to-all-start = ((f32[128,4,128]{2,1,0:T(4,128)}), f32[128,4,128]{2,1,0:T(4,128)S(1)}, u32[]{:S(2)}, u32[]{:S(2)}) async-start(f32[128,4,128]{2,1,0:T(4,128)} %bitcast.17), calls=%async_computation | async-start | bytes 524288 | tf_op jit(solution)/shard_map/all_to_all | solution.py:418
  129.0 0.8 copy-start.7
  129.0 0.8 copy-start.8
  129.1 10.9 %copy-start = (s32[16,4,128]{2,1,0:T(4,128)S(1)}, s32[16,4,128]{2,1,0:T(4,128)}, u32[]{:S(2)}) copy-start(s32[16,4,128]{2,1,0:T(4,128)} %col.1) | copy-start | bytes 98308
  129.1 10.9 %copy-start.1 = (s32[2,128]{1,0:T(2,128)S(1)}, s32[2,128]{1,0:T(2,128)}, u32[]{:S(2)}) copy-start(s32[2,128]{1,0:T(2,128)} %support.1) | copy-start | bytes 3076
  140.0 4.7 %copy-start.3 = (f32[3,1024,128]{2,1,0:T(8,128)S(1)}, f32[3,1024,128]{2,1,0:T(8,128)}, u32[]{:S(2)}) copy-start(f32[3,1024,128]{2,1,0:T(8,128)} %get-tuple-element.9) | copy-start | bytes 4718596
  144.7 2.0 %copy-start.2 = (f32[3,1024,128]{2,1,0:T(8,128)S(1)}, f32[3,1024,128]{2,1,0:T(8,128)}, u32[]{:S(2)}) copy-start(f32[3,1024,128]{2,1,0:T(8,128)} %get-tuple-element.10) | copy-start | bytes 4718596

commit v2 on v1

--- a/solution.py
+++ b/solution.py
@@ -14,7 +14,7 @@
 STEPS = 10
 GX, GY = 8, 16
 R = 144
-GR = 4
+GR = 3
 VMEM = pltpu.VMEM
 
 
@@ -64,7 +64,9 @@
     wv = full([lap, dx])
     wv0 = np.concatenate([inner([dz]), select(1)], 1)
     wsel = np.stack([select(0), select(2)])
-    return [jnp.asarray(a.astype(ml_dtypes.bfloat16)) for a in (wu, ww, ww0, wv, wv0, wsel)]
+    k, n = np.arange(128)[:, None], np.arange(128)[None, :]
+    wslot = np.stack([two(((n == k // 4 * 4 + s) & (k < 120)).astype(np.float32)) for s in range(4)])
+    return [jnp.asarray(a.astype(ml_dtypes.bfloat16)) for a in (wu, ww, ww0, wv, wv0, wsel, wslot)]
 
 
 def d1(m2, m1, p1, p2):
@@ -72,9 +74,10 @@
 
 
 def wave_kernel(
-    now, prev, shear, bulk, found, wu, ww, ww0, wv, wv0, wsel,
+    now, prev, shear, bulk, found, wu, ww, ww0, wv, wv0, wsel, wslot,
     out_now, out_prev, out_ground,
-    WA, WB, SB, BH, MU, HU, HIST, PS, PR, send_sem, recv_sem,
+    WA, WB, SB, BH, BHE, MU, HIST, PS, PR, G1, A1, B1, out_rows,
+    send_sem, recv_sem, send_y, recv_y, send_x, recv_x,
 ):
     gx, gy = lax.axis_index("gx"), lax.axis_index("gy")
 
@@ -89,11 +92,16 @@
         W[...] = jnp.zeros_like(W)
     PR[...] = jnp.zeros_like(PR)
     BH[...] = jnp.zeros_like(BH)
+    BHE[...] = jnp.zeros_like(BHE)
     HIST[...] = jnp.zeros_like(HIST)
 
     barrier = pltpu.get_barrier_semaphore()
-    count = 0
-    for dx, dy in dirs:
+    count = (GX - 1) + (GY - 1)
+    for i in range(1, GX):
+        pl.semaphore_signal(barrier, inc=1, device_id={"gx": (gx + i) % GX, "gy": gy}, device_id_type=MESH)
+    for i in range(1, GY):
+        pl.semaphore_signal(barrier, inc=1, device_id={"gx": gx, "gy": (gy + i) % GY}, device_id_type=MESH)
+    for dx, dy in dirs[4:]:
         ok = has(dx, dy)
         count = count + ok.astype(jnp.int32)
 
@@ -139,18 +147,24 @@
             device_id={"gx": gx + dx, "gy": gy + dy}, device_id_type=MESH,
         )
 
-    def send(p):
+    X_DIRS, Y_DIRS = (0, 1, 4, 5, 6, 7), (2, 3)
+
+    def start(p, which):
+        for d in which:
+            dx, dy = dirs[d]
+
+            @pl.when(has(dx, dy))
+            def _():
+                copy(p, d).start()
+
+    def send_edges_x(p):
         W = WS[p]
         for c in range(3):
             low, high = W[c, 8, 8:72, :], W[c, 8, 72:136, :]
             PS[p, 1, c] = jnp.where(lane < 64, pltpu.roll(low, 64, 1), high)
             low, high = W[c, 1, 8:72, :], W[c, 1, 72:136, :]
             PS[p, 0, c] = jnp.where(lane < 64, low, pltpu.roll(high, 64, 1))
-        for d, (dx, dy) in enumerate(dirs):
-
-            @pl.when(has(dx, dy))
-            def _():
-                copy(p, d).start()
+        start(p, X_DIRS)
 
     def finish(p):
         for d, (dx, dy) in enumerate(dirs):
@@ -173,138 +187,180 @@
             W[c, 9, 8:72, :] = right
             W[c, 9, 72:136, :] = pltpu.roll(right, 64, 1)
 
-    def split_slab(W, c, xs, own=True, up=True, down=True):
-        x = W[c, xs]
+    def halves(x):
         hi = x.astype(BF)
-        lo = (x - hi.astype(F32)).astype(BF)
-        at = xs * R if isinstance(xs, int) else pl.multiple_of(xs * R, R)
-        if own:
-            BH[c, pl.ds(at, R), 0:128] = hi
-            BH[c, pl.ds(at, R), 128:256] = lo
-        if up:
-            BH[c, pl.ds(at + R, R), 320:384] = hi[:, 64:128]
-            BH[c, pl.ds(at + R, R), 448:512] = lo[:, 64:128]
-        if down:
-            BH[c, pl.ds(at - R, R), 256:320] = hi[:, 0:64]
-            BH[c, pl.ds(at - R, R), 384:448] = lo[:, 0:64]
-
-    def split_all(W):
-        def body(xs, _):
+        return hi, (x - hi.astype(F32)).astype(BF)
+
+    def put(B, c, x, own, up, down, n):
+        hi, lo = halves(x)
+        if own is not None:
+            B[c, pl.ds(own, n), 0:128] = hi
+            B[c, pl.ds(own, n), 128:256] = lo
+        if up is not None:
+            B[c, pl.ds(up, n), 320:384] = hi[:, 64:128]
+            B[c, pl.ds(up, n), 448:512] = lo[:, 64:128]
+        if down is not None:
+            B[c, pl.ds(down, n), 256:320] = hi[:, 0:64]
+            B[c, pl.ds(down, n), 384:448] = lo[:, 0:64]
+
+    def split_inner(W):
+        def body(i, _):
+            own = pl.multiple_of(i * 128, 128)
+            up = pl.multiple_of(i * 128 + 128, 128)
+            down = pl.multiple_of(lax.rem(i + 7, 8) * 128, 128)
             for c in range(3):
-                split_slab(W, c, xs + 1)
+                put(BH, c, W[c, i + 2, 8:136, :], own, up, down, 128)
             return 0
 
-        lax.fori_loop(0, 8, body, 0)
+        lax.fori_loop(0, 6, body, 0)
         for c in range(3):
-            split_slab(W, c, 0, own=False, down=False)
-            split_slab(W, c, 9, own=False, up=False)
+            put(BH, c, W[c, 8, 8:136, :], 6 * 128, None, 5 * 128, 128)
+            put(BH, c, W[c, 1, 8:136, :], 7 * 128, 0, None, 128)
+
+    def split_halo(W):
+        for c in range(3):
+            put(BH, c, W[c, 0, 8:136, :], None, 7 * 128, None, 128)
+            put(BH, c, W[c, 9, 8:136, :], None, None, 6 * 128, 128)
+            for xs in range(10):
+                if c == 2 and xs in (0, 9):
+                    continue
+                edge = jnp.concatenate([W[c, xs, 0:8, :], W[c, xs, 136:144, :]], 0)
+                at = (xs - 1) * 16
+                inside = 1 <= xs <= 8
+                cross = c < 2
+                put(
+                    BHE, c, edge,
+                    at if inside else None,
+                    at + 16 if xs <= 7 and cross else None,
+                    at - 16 if xs >= 2 and cross else None,
+                    16,
+                )
 
     dot = functools.partial(jnp.dot, preferred_element_type=F32)
-    n = GR * R
-
-    def matmuls(g):
-        at = pl.multiple_of(g * n + R, R)
+
+    def matmuls(at, n, store, surf):
         u = dot(BH[0, pl.ds(at, n), :], wu[...])
         w = dot(BH[2, pl.ds(at, n), :], ww[...])
         w0 = dot(BH[2, pl.ds(at, n), 0:256], ww0[...])
         v = dot(BH[1, pl.ds(at, n), :], wv[...])
         v0 = dot(BH[1, pl.ds(at, n), 0:256], wv0[...])
-        part = lambda a: a.reshape(GR, R, 128)
-        MU[0] = part(u[:, 0:128])
-        MU[1] = part(v[:, 0:128])
-        MU[2] = part(w[:, 0:128])
-        MU[3] = part(u[:, 128:256] + w[:, 128:256])
-        MU[4] = part(u[:, 256:384] + w0[:, 0:128])
-        MU[5] = part(u[:, 384:512] + w0[:, 128:256])
-        MU[6] = part(v[:, 128:256])
-        MU[7] = part(v0[:, 0:128])
-        return v0[:, 128:256]
-
-    def surface(g, picked, t):
-        at = pl.multiple_of(g * n + R, R)
-        picked = picked + dot(BH[0, pl.ds(at, n), 0:256], wsel[0]) + dot(BH[2, pl.ds(at, n), 0:256], wsel[1])
-        group = lax.broadcasted_iota(jnp.int32, (GR, 128, 128), 2) // 12
-        where = pl.ds(g * GR, GR)
-        HIST[where] = jnp.where(group == t, picked.reshape(GR, R, 128)[:, 8:136, :], HIST[where])
-
-    def update(g, j, W, N):
-        xs = g * GR + j
+        store(0, u[:, 0:128])
+        store(1, v[:, 0:128])
+        store(2, w[:, 0:128])
+        store(3, u[:, 128:256] + w[:, 128:256])
+        store(4, u[:, 256:384] + w0[:, 0:128])
+        store(5, u[:, 384:512] + w0[:, 128:256])
+        store(6, v[:, 128:256])
+        store(7, v0[:, 0:128])
+        surf(v0[:, 128:256] + dot(BH[0, pl.ds(at, n), 0:256], wsel[0]) + dot(BH[2, pl.ds(at, n), 0:256], wsel[1]))
+
+    group = lax.broadcasted_iota(jnp.int32, (128, 128), 1) // 12
+
+    def keep_surface(t, xs, a):
+        HIST[xs - 1] = jnp.where(group == t, a, HIST[xs - 1])
+
+    def edge_matmuls():
+        wdx, wdz = wu[:, 384:512], ww0[:, 128:256]
+        e = dot(BHE[0], wdx) + dot(BHE[2, :, 0:256], wdz)
+        f = dot(BHE[1], wdx)
+        g = dot(BHE[1, :, 0:256], wdz)
+        for k, a in ((5, e), (6, f), (7, g)):
+            a = a.reshape(8, 16, 128)
+            MU[k, :, 0:8, :] = a[:, 0:8]
+            MU[k, :, 136:144, :] = a[:, 8:16]
+
+    def update(xs, blocks, W, N):
+        j = xs - 1
         D = (-2, -1, 1, 2)
-        for yb in range(16):
+        for yb in blocks:
             r = lambda d: pl.ds(8 + yb * 8 + d, 8)
-            sh = SB[0, xs, yb * 8 : yb * 8 + 8, :]
-            bu = SB[1, xs, yb * 8 : yb * 8 + 8, :]
+            sh = SB[0, j, yb * 8 : yb * 8 + 8, :]
+            bu = SB[1, j, yb * 8 : yb * 8 + 8, :]
             mix = [
                 MU[3, j, r(0), :] + d1(*[MU[6, j, r(d), :] for d in D]),
                 d1(*[MU[5, j, r(d), :] for d in D]),
                 MU[4, j, r(0), :] + d1(*[MU[7, j, r(d), :] for d in D]),
             ]
             for c in range(3):
-                y = [W[c, xs + 1, r(d), :] for d in D]
-                mid = W[c, xs + 1, r(0), :]
+                y = [W[c, xs, r(d), :] for d in D]
+                mid = W[c, xs, r(0), :]
                 dyy = 16.0 * (y[1] + y[2]) - (y[0] + y[3]) - 30.0 * mid
                 lap = MU[c, j, r(0), :] + dyy
                 b = mix[c] + 12.0 * dyy if c == 1 else mix[c]
-                N[c, xs + 1, r(0), :] = (2.0 * mid - N[c, xs + 1, r(0), :]) + (sh * lap + bu * b)
-
-    def substep(p, t):
+                N[c, xs, r(0), :] = (2.0 * mid - N[c, xs, r(0), :]) + (sh * lap + bu * b)
+
+    def substep(p, t, send_after):
         W, N = WS[p], WS[1 - p]
+        split_inner(W)
+
+        def body(g, _):
+            def store(k, a):
+                MU[k, pl.ds(g * GR + 1, GR), 8:136, :] = a.reshape(GR, 128, 128)
+
+            def surf(a):
+                for i in range(GR):
+                    keep_surface(t, g * GR + 2 + i, a[128 * i : 128 * i + 128])
+
+            matmuls(pl.multiple_of(g * (GR * 128), 128), GR * 128, store, surf)
+            for i in range(GR):
+                update(g * GR + 2 + i, range(1, 15), W, N)
+            return 0
+
+        lax.fori_loop(0, 6 // GR, body, 0)
         finish(p)
-        split_all(W)
-
-        def body(g, _):
-            picked = matmuls(g)
-            surface(g, picked, t)
-            for j in range(GR):
-                update(g, j, W, N)
+        split_halo(W)
+
+        def store(k, a):
+            MU[k, 7, 8:136, :] = a[0:128]
+            MU[k, 0, 8:136, :] = a[128:256]
+
+        def surf(a):
+            keep_surface(t, 8, a[0:128])
+            keep_surface(t, 1, a[128:256])
+
+        matmuls(6 * 128, 256, store, surf)
+        edge_matmuls()
+        update(1, range(16), W, N)
+        update(8, range(16), W, N)
+
+        def when_more(f):
+            if send_after is True:
+                f()
+            else:
+                pl.when(send_after)(f)
+
+        when_more(lambda: send_edges_x(1 - p))
+
+        def body_y(i, _):
+            update(i + 2, (0, 15), W, N)
             return 0
 
-        lax.fori_loop(0, 8 // GR, body, 0)
-
-    send(0)
+        lax.fori_loop(0, 6, body_y, 0)
+        when_more(lambda: start(1 - p, Y_DIRS))
+
+    send_edges_x(0)
+    start(0, Y_DIRS)
 
     def pair(i, _):
-        substep(0, 2 * i - 1)
-        send(1)
-        substep(1, 2 * i)
-
-        @pl.when(i < STEPS // 2 - 1)
-        def _():
-            send(0)
-
+        substep(0, 2 * i - 1, True)
+        substep(1, 2 * i, i < STEPS // 2 - 1)
         return 0
 
     lax.fori_loop(0, STEPS // 2, pair, 0)
 
-    def last(xs, _):
+    def last(i, _):
+        total = jnp.zeros((128, 128), F32)
         for c in range(3):
-            split_slab(WA, c, xs + 1, up=False, down=False)
+            w = wv0[:, 128:256] if c == 1 else wsel[c // 2]
+            total = total + dot(jnp.concatenate(halves(WA[c, i + 1, 8:136, :]), 1), w)
+        keep_surface(STEPS - 1, i + 1, total)
         return 0
 
     lax.fori_loop(0, 8, last, 0)
 
-    def last_surface(g, _):
-        at = pl.multiple_of(g * n + R, R)
-        surface(g, dot(BH[1, pl.ds(at, n), 0:256], wv0[:, 128:256]), STEPS - 1)
-        return 0
-
-    lax.fori_loop(0, 8 // GR, last_surface, 0)
-
-    cell = found[...]
-    row = (cell // 512) * 128 + cell % 128
-    quarter = (cell // 128) % 4
-    total = jnp.zeros((512, 256), F32)
-    for i in range(4):
-        pick = (row == lax.broadcasted_iota(jnp.int32, (512, 256), 1) + 256 * i).astype(F32).astype(BF)
-        h = HIST[2 * i : 2 * i + 2].reshape(256, 128)
-        hi = h.astype(BF)
-        lo = (h - hi.astype(F32)).astype(BF)
-        total = total + dot(pick, jnp.concatenate([hi, lo], 1))
-    keep = lax.broadcasted_iota(jnp.int32, (512, 128), 1) % 4 == quarter
-    out_ground[...] = jnp.where(keep, total[:, 0:128] + total[:, 128:256], 0.0)
-
-    for c in range(3):
-        for dst, W in ((out_now, WA), (out_prev, WB)):
+    def store_fields(which):
+        dst, W = ((out_now, WA), (out_prev, WB))[which]
+        for c in range(3):
 
             def store_field(xs, _):
                 m = W[c, xs + 1, 8:136, :].T
@@ -315,30 +371,85 @@
 
             lax.fori_loop(0, 8, store_field, 0)
 
+    cells = jnp.concatenate([found[...].astype(F32), jnp.zeros((124, 128), F32)], 0).T.astype(jnp.int32)
+    rows = jnp.zeros((128, 128), F32)
+    wide = lax.broadcasted_iota(jnp.int32, (128, 256), 1)
+    narrow = lax.broadcasted_iota(jnp.int32, (128, 128), 1)
+    for s in range(4):
+        cell = cells[:, s : s + 1]
+        row = (cell // 512) * 128 + cell % 128
+        quarter = (cell // 128) % 4
+        total = jnp.zeros((128, 256), F32)
+        for i in range(4):
+            pick = (row == wide + 256 * i).astype(F32).astype(BF)
+            h = HIST[2 * i : 2 * i + 2].reshape(256, 128)
+            total = total + dot(pick, jnp.concatenate(halves(h), 1))
+        got = jnp.where(narrow % 4 == quarter, total[:, 0:128] + total[:, 128:256], 0.0)
+        rows = rows + dot(jnp.concatenate(halves(got), 1), wslot[s])
+    for i in range(GX):
+        G1[:, i, :] = rows[GY * i : GY * i + GY]
+
+    def over_y(i):
+        to = (gy + i) % GY
+        return pltpu.make_async_remote_copy(
+            src_ref=G1.at[to], dst_ref=A1.at[gy], send_sem=send_y.at[i], recv_sem=recv_y.at[i],
+            device_id={"gx": gx, "gy": to}, device_id_type=MESH,
+        )
+
+    def over_x(i):
+        to = (gx + i) % GX
+        return pltpu.make_async_remote_copy(
+            src_ref=B1.at[to], dst_ref=out_rows.at[gx], send_sem=send_x.at[i], recv_sem=recv_x.at[i],
+            device_id={"gx": to, "gy": gy}, device_id_type=MESH,
+        )
+
+    for i in range(1, GY):
+        over_y(i).start()
+    A1[gy] = G1[gy]
+    store_fields(0)
+    for i in range(1, GY):
+        over_y(i).wait()
+    for i in range(GX):
+        B1[i] = A1[:, i, :]
+    for i in range(1, GX):
+        over_x(i).start()
+    out_rows[gx] = B1[gx]
+    store_fields(1)
+    for i in range(1, GX):
+        over_x(i).wait()
+    out_ground[...] = out_rows[...]
+
 
 def bridge_kernel(
-    received, support, col, val_hbm, mass, disp, vel, acc,
-    out_disp, out_vel,
-    val, ground, state, sem,
+    received, support, col, val_hbm, mass, disp, vel, acc, now, before,
+    out_disp, out_vel, out_now, out_before,
+    val, ground, state, sem, pass_sem,
 ):
     copies = []
     for node in range(16):
         c = pltpu.make_async_copy(val_hbm.at[node], val.at[:, :, :, node, :], sem.at[node])
         c.start()
         copies.append(c)
-    rows = lax.broadcasted_iota(jnp.int32, (512, 128), 0)
-    pick = jnp.concatenate([(rows == support[k : k + 1, :]).astype(F32).astype(BF) for k in range(2)], 1)
-    flat = jnp.concatenate([received[128 * i : 128 * i + 128, :].T for i in range(4)], 1)
+    passed = []
+    for i, (src, dst) in enumerate(((now, out_now), (before, out_before))):
+        c = pltpu.make_async_copy(src, dst, pass_sem.at[i])
+        c.start()
+        passed.append(c)
+    rows = jnp.concatenate([support[0:1, :], support[1:2, :]], 1)
+    pick = (lax.broadcasted_iota(jnp.int32, (128, 256), 0) == rows // 4).astype(F32).astype(BF)
+    flat = received[...].T
     hi = flat.astype(BF)
     lo = (flat - hi.astype(F32)).astype(BF)
     dot = functools.partial(jnp.dot, preferred_element_type=F32)
-    ground[...] = jnp.sum((dot(hi, pick) + dot(lo, pick)).reshape(32, 4, 256), axis=1, keepdims=True)
+    found = dot(hi, pick) + dot(lo, pick)
+    slot = lax.broadcasted_iota(jnp.int32, (128, 256), 0) % 4 == rows % 4
+    ground[...] = jnp.sum(jnp.where(slot, found, 0.0).reshape(32, 4, 256), axis=1, keepdims=True)
     D, V, A = 0, 6, 12
     for d in range(6):
-        state[D + d] = disp[:, d, :]
-        state[V + d] = vel[:, d, :]
-        state[A + d] = acc[:, d, :]
-        state[18 + d] = mass[:, d, :]
+        state[D + d] = disp[d]
+        state[V + d] = vel[d]
+        state[A + d] = acc[d]
+        state[18 + d] = mass[d]
     for c in copies:
         c.wait()
     sub = lax.broadcasted_iota(jnp.int32, (16, 128), 0)
@@ -361,7 +472,7 @@
                         halves.append(jnp.where(ix >= 8, g1, g0))
                     v = jnp.concatenate(halves, 0)
                 for e in range(6):
-                    total[e] = total[e] + val[j, e, d] * v
+                    total[e] = total[e] + val[e, d, j] * v
         for d in range(6):
             force = -total[d]
             if d < 3:
@@ -375,8 +486,10 @@
 
     lax.fori_loop(0, STEPS, step, 0)
     for d in range(6):
-        out_disp[:, d, :] = state[D + d]
-        out_vel[:, d, :] = state[V + d]
+        out_disp[d] = state[D + d]
+        out_vel[d] = state[V + d]
+    for c in passed:
+        c.wait()
 
 
 def local(
@@ -390,22 +503,30 @@
         out_shape=[
             jax.ShapeDtypeStruct((3, 1024, 128), F32),
             jax.ShapeDtypeStruct((3, 1024, 128), F32),
-            jax.ShapeDtypeStruct((512, 128), F32),
+            jax.ShapeDtypeStruct((GX, GY, 128), F32),
         ],
-        in_specs=[vm] * 11,
+        in_specs=[vm] * 12,
         out_specs=[vm] * 3,
         scratch_shapes=[
             VMEM((3, 10, R, 128), F32),
             VMEM((3, 10, R, 128), F32),
             VMEM((2, 8, 128, 128), F32),
-            VMEM((3, 10 * R, 512), BF),
-            VMEM((8, GR, R, 128), F32),
-            VMEM((8, 128), F32),
+            VMEM((3, 1024, 512), BF),
+            VMEM((3, 128, 512), BF),
+            VMEM((8, 8, R, 128), F32),
             VMEM((8, 128, 128), F32),
             VMEM((2, 2, 3, 64, 128), F32),
             VMEM((2, 2, 3, 64, 128), F32),
+            VMEM((GY, GX, 128), F32),
+            VMEM((GY, GX, 128), F32),
+            VMEM((GX, GY, 128), F32),
+            VMEM((GX, GY, 128), F32),
             pltpu.SemaphoreType.DMA((2, 8)),
             pltpu.SemaphoreType.DMA((2, 8)),
+            pltpu.SemaphoreType.DMA((GY,)),
+            pltpu.SemaphoreType.DMA((GY,)),
+            pltpu.SemaphoreType.DMA((GX,)),
+            pltpu.SemaphoreType.DMA((GX,)),
         ],
         compiler_params=pltpu.CompilerParams(
             collective_id=0, has_side_effects=True, vmem_limit_bytes=56 * 2**20
@@ -413,25 +534,29 @@
     )(
         wave_now.reshape(3, 1024, 128), wave_prev.reshape(3, 1024, 128),
         shear_mod.reshape(1024, 128), bulk_mod.reshape(1024, 128),
-        found_cell.reshape(512, 1), *weights,
+        found_cell.reshape(128, 4).T, *weights,
     )
-    received = lax.all_to_all(
-        outgoing.reshape(128, 4, 128), ("gx", "gy"), split_axis=0, concat_axis=0, tiled=True
-    ).reshape(512, 128)
-    deck_disp, deck_vel = pl.pallas_call(
+    by_dof = lambda a: jnp.transpose(a, (1, 0, 2))
+    hbm = pl.BlockSpec(memory_space=pl.ANY)
+    field = jax.ShapeDtypeStruct((3, 1024, 128), F32)
+    deck_disp, deck_vel, now, before = pl.pallas_call(
         bridge_kernel,
-        out_shape=[jax.ShapeDtypeStruct((16, 6, 128), F32)] * 2,
-        in_specs=[vm] * 3 + [pl.BlockSpec(memory_space=pl.ANY)] + [vm] * 4,
-        out_specs=[vm] * 2,
+        out_shape=[jax.ShapeDtypeStruct((6, 16, 128), F32)] * 2 + [field] * 2,
+        in_specs=[vm] * 3 + [hbm] + [vm] * 4 + [hbm] * 2,
+        out_specs=[vm] * 2 + [hbm] * 2,
         scratch_shapes=[
-            VMEM((4, 6, 6, 16, 128), F32),
+            VMEM((6, 6, 4, 16, 128), F32),
             VMEM((32, 1, 256), F32),
             VMEM((24, 16, 128), F32),
             pltpu.SemaphoreType.DMA((16,)),
+            pltpu.SemaphoreType.DMA((2,)),
         ],
         compiler_params=pltpu.CompilerParams(vmem_limit_bytes=32 * 2**20),
-    )(received, support_row, block_col, block_val, mass_inv, bridge_disp, bridge_vel, bridge_acc)
-    return now.reshape(3, 32, 32, 128), before.reshape(3, 32, 32, 128), deck_disp, deck_vel
+    )(
+        outgoing.reshape(128, 128), support_row, block_col, jnp.transpose(block_val, (0, 2, 3, 1, 4)),
+        by_dof(mass_inv), by_dof(bridge_disp), by_dof(bridge_vel), by_dof(bridge_acc), now, before,
+    )
+    return now.reshape(3, 32, 32, 128), before.reshape(3, 32, 32, 128), by_dof(deck_disp), by_dof(deck_vel)
 
 
 def solution(mesh):

time: 148 us -> 106 us (0.72)
  Pallas kernels: 119 us -> 101 us
  starting transfers between devices: 11.2 us -> 0 us
  waiting for transfers between devices: 10.1 us -> 0 us
  local copies, waits for them, and re-layouts: 6.77 us -> 3.68 us
    pallas_call x1, Pallas kernels: 116 us -> 97.5 us  [local(): pl.pallas_call(wave_kernel, out_shape=[jax.ShapeDtypeStruct((3, 1024, 128...]
    all_to_all x1 -> x0, starting transfers between devices: 11.2 us -> none  [local(): lax.all_to_all(outgoing.reshape(128, 4, 128), ('gx', 'gy'), split_axis=0,...]
    all_to_all x1 -> x0, waiting for transfers between devices: 10.1 us -> none  [local(): lax.all_to_all(outgoing.reshape(128, 4, 128), ('gx', 'gy'), split_axis=0,...]
    unnamed x28 -> x20, local copies, waits for them, and re-layouts: 5.95 us -> 3.68 us
  transfers between devices with their start and end apart: 1 -> 0, of which waited for: 1 -> 0; matrix products, arithmetic and copies ran while one was open for 0% -> 0% of each run, Pallas kernels for 0% -> 0%
where the time goes in v2:
time: 106 us
  Pallas kernels  101 us (95%)
  local copies, waits for them, and re-layouts  3.68 us (3%)
    pallas_call x1, Pallas kernels, local(): pl.pallas_call(wave_kernel, out_shape=[jax.ShapeDtypeStruct((3, 1024, 128...  97.5 us
    pallas_call x1, Pallas kernels, local(): pl.pallas_call(bridge_kernel, out_shape=[jax.ShapeDtypeStruct((6, 16, 128...  3.87 us
    unnamed x20, local copies, waits for them, and re-layouts  3.68 us

profile of v2, /device:TPU:1, one launch (start us, length us, event | category | flops | bytes accessed | tf_op | source)
XLA Modules:
  0.0 105.8 jit_solution(9364765200237220811)
XLA Ops:
  0.6 0.0 copy-start.2
  0.6 0.0 copy-start.4
  0.7 0.0 copy-start.5
  0.7 0.0 copy-start.6
  0.7 0.0 copy-start.7
  0.7 0.0 copy-start.8
  0.7 0.0 copy-start.9
  0.7 97.5 %shard_map.210 = (f32[3,1024,128]{2,1,0:T(8,128)}, f32[3,1024,128]{2,1,0:T(8,128)}, f32[8,16,128]{2,1,0:T(8,128)}) custom-call(f32[3,1024,128]{2,1,0:T(8,128)} %bitcast.23, f32[3,1024,128]{2,1,0:T(8,128)} %bitcast.24, f32[1024,128]{1,0:T(8,128)} %bitcast.25, f32[1024,128]{1,0:T(8,128)} %bitcast.26, s32[4,128]{1,0:T(4,128)} %bitcast.27, ...), custom_call_target="tpu_custom_call" | custom-call | tf_op jit(solution)/shard_map/pallas_call | solution.py:501
  98.2 0.0 copy-done.2
  98.2 0.0 copy-done.4
  98.2 0.0 copy-done.5
  98.2 0.0 copy-done.6
  98.3 0.0 copy-done.7
  98.3 0.0 copy-done.8
  98.3 0.0 copy-done.9
  98.3 0.0 copy-start
  98.3 1.4 %copy-done = f32[3,1024,128]{2,1,0:T(8,128)S(1)} copy-done((f32[3,1024,128]{2,1,0:T(8,128)S(1)}, f32[3,1024,128]{2,1,0:T(8,128)}, u32[]{:S(2)}) %copy-start) | copy-done | bytes 1572888
  99.7 0.0 copy-start.1
  99.7 1.4 %copy-done.1 = f32[3,1024,128]{2,1,0:T(8,128)S(1)} copy-done((f32[3,1024,128]{2,1,0:T(8,128)S(1)}, f32[3,1024,128]{2,1,0:T(8,128)}, u32[]{:S(2)}) %copy-start.1) | copy-done | bytes 1572888
  101.1 0.0 copy-start.3
  101.1 0.8 copy-done.3
  101.9 3.9 %shard_map.211 = (f32[6,16,128]{2,1,0:T(8,128)}, f32[6,16,128]{2,1,0:T(8,128)}, f32[3,1024,128]{2,1,0:T(8,128)}, f32[3,1024,128]{2,1,0:T(8,128)}) custom-call(f32[128,128]{1,0:T(8,128)S(1)} %bitcast.18, s32[2,128]{1,0:T(2,128)S(1)} %copy-done.9, s32[16,4,128]{2,1,0:T(4,128)S(1)} %copy-done.8, f32[16,6,6,4,128]{4,3,2,1,0:T(4,128)S(1)} %bitcast.17, ...), custom_call_target="tpu_custom_call" | custom-call | tf_op jit(solution)/shard_map/pallas_call | solution.py:542
Async XLA Ops:
  0.6 97.6 %copy-start.2 = (f32[16,4,6,6,128]{4,1,3,2,0:T(4,128)S(1)}, f32[16,4,6,6,128]{4,1,3,2,0:T(4,128)}, u32[]{:S(2)}) copy-start(f32[16,4,6,6,128]{4,1,3,2,0:T(4,128)} %param.26) | copy-start | bytes 3538948
  0.6 97.6 %copy-start.4 = (f32[16,6,128]{2,0,1:T(8,128)S(1)}, f32[16,6,128]{2,0,1:T(8,128)}, u32[]{:S(2)}) copy-start(f32[16,6,128]{2,0,1:T(8,128)} %param.27) | copy-start | bytes 147460
  0.7 97.6 %copy-start.5 = (f32[16,6,128]{2,0,1:T(8,128)S(1)}, f32[16,6,128]{2,0,1:T(8,128)}, u32[]{:S(2)}) copy-start(f32[16,6,128]{2,0,1:T(8,128)} %param.28) | copy-start | bytes 147460
  0.7 97.6 %copy-start.6 = (f32[16,6,128]{2,0,1:T(8,128)S(1)}, f32[16,6,128]{2,0,1:T(8,128)}, u32[]{:S(2)}) copy-start(f32[16,6,128]{2,0,1:T(8,128)} %param.29) | copy-start | bytes 147460
  0.7 97.6 %copy-start.7 = (f32[16,6,128]{2,0,1:T(8,128)S(1)}, f32[16,6,128]{2,0,1:T(8,128)}, u32[]{:S(2)}) copy-start(f32[16,6,128]{2,0,1:T(8,128)} %param.30) | copy-start | bytes 147460
  0.7 97.6 %copy-start.8 = (s32[16,4,128]{2,1,0:T(4,128)S(1)}, s32[16,4,128]{2,1,0:T(4,128)}, u32[]{:S(2)}) copy-start(s32[16,4,128]{2,1,0:T(4,128)} %col.1) | copy-start | bytes 98308
  0.7 97.6 %copy-start.9 = (s32[2,128]{1,0:T(2,128)S(1)}, s32[2,128]{1,0:T(2,128)}, u32[]{:S(2)}) copy-start(s32[2,128]{1,0:T(2,128)} %support.1) | copy-start | bytes 3076
  98.3 1.4 %copy-start = (f32[3,1024,128]{2,1,0:T(8,128)S(1)}, f32[3,1024,128]{2,1,0:T(8,128)}, u32[]{:S(2)}) copy-start(f32[3,1024,128]{2,1,0:T(8,128)} %get-tuple-element.12.now) | copy-start | bytes 4718596
  99.7 1.4 %copy-start.1 = (f32[3,1024,128]{2,1,0:T(8,128)S(1)}, f32[3,1024,128]{2,1,0:T(8,128)}, u32[]{:S(2)}) copy-start(f32[3,1024,128]{2,1,0:T(8,128)} %get-tuple-element.13.before) | copy-start | bytes 4718596
  101.1 0.8 copy-start.3

commit v3 on v2

--- a/solution.py
+++ b/solution.py
@@ -89,10 +89,11 @@
     lane = lax.broadcasted_iota(jnp.int32, (64, 128), 1)
 
     for W in WS:
-        W[...] = jnp.zeros_like(W)
+        for xs in (0, 9):
+            W[:, xs] = jnp.zeros((3, R, 128), F32)
+        for y in (0, 136):
+            W[:, 1:9, y : y + 8, :] = jnp.zeros((3, 8, 8, 128), F32)
     PR[...] = jnp.zeros_like(PR)
-    BH[...] = jnp.zeros_like(BH)
-    BHE[...] = jnp.zeros_like(BHE)
     HIST[...] = jnp.zeros_like(HIST)
 
     barrier = pltpu.get_barrier_semaphore()
@@ -147,45 +148,38 @@
             device_id={"gx": gx + dx, "gy": gy + dy}, device_id_type=MESH,
         )
 
-    X_DIRS, Y_DIRS = (0, 1, 4, 5, 6, 7), (2, 3)
-
-    def start(p, which):
-        for d in which:
-            dx, dy = dirs[d]
-
-            @pl.when(has(dx, dy))
-            def _():
-                copy(p, d).start()
-
-    def send_edges_x(p):
+    def each(dx, step):
+        for d, (ex, ey) in enumerate(dirs):
+            if ex == dx:
+                pl.when(has(ex, ey) if step != "recv" else has(-ex, -ey))(functools.partial(act, d, step))
+
+    def act(d, step):
+        c = copy(act.p, d)
+        if step == "start":
+            c.start()
+        elif step == "recv":
+            c.wait_recv()
+        else:
+            c.wait_send()
+
+    def start(p, dx):
+        act.p = p
+        each(dx, "start")
+
+    def wait(p, dx_recv, dx_send):
+        act.p = p
+        each(dx_recv, "recv")
+        each(dx_send, "send")
+
+    def send_side(p, xs):
         W = WS[p]
         for c in range(3):
-            low, high = W[c, 8, 8:72, :], W[c, 8, 72:136, :]
-            PS[p, 1, c] = jnp.where(lane < 64, pltpu.roll(low, 64, 1), high)
-            low, high = W[c, 1, 8:72, :], W[c, 1, 72:136, :]
-            PS[p, 0, c] = jnp.where(lane < 64, low, pltpu.roll(high, 64, 1))
-        start(p, X_DIRS)
-
-    def finish(p):
-        for d, (dx, dy) in enumerate(dirs):
-
-            @pl.when(has(-dx, -dy))
-            def _():
-                copy(p, d).wait_recv()
-
-        for d, (dx, dy) in enumerate(dirs):
-
-            @pl.when(has(dx, dy))
-            def _():
-                copy(p, d).wait_send()
-
-        W = WS[p]
-        for c in range(3):
-            left, right = PR[p, 0, c], PR[p, 1, c]
-            W[c, 0, 8:72, :] = pltpu.roll(left, 64, 1)
-            W[c, 0, 72:136, :] = left
-            W[c, 9, 8:72, :] = right
-            W[c, 9, 72:136, :] = pltpu.roll(right, 64, 1)
+            low, high = W[c, xs, 8:72, :], W[c, xs, 72:136, :]
+            if xs == 8:
+                PS[p, 1, c] = jnp.where(lane < 64, pltpu.roll(low, 64, 1), high)
+            else:
+                PS[p, 0, c] = jnp.where(lane < 64, low, pltpu.roll(high, 64, 1))
+        start(p, 1 if xs == 8 else -1)
 
     def halves(x):
         hi = x.astype(BF)
@@ -203,38 +197,48 @@
             B[c, pl.ds(down, n), 256:320] = hi[:, 0:64]
             B[c, pl.ds(down, n), 384:448] = lo[:, 0:64]
 
-    def split_inner(W):
+    BASE = {8: 768, 1: 912}
+
+    def split_own(W):
         def body(i, _):
             own = pl.multiple_of(i * 128, 128)
             up = pl.multiple_of(i * 128 + 128, 128)
-            down = pl.multiple_of(lax.rem(i + 7, 8) * 128, 128)
+            down = pl.multiple_of(jnp.where(i == 0, BASE[1], i * 128 - 128), 16)
             for c in range(3):
                 put(BH, c, W[c, i + 2, 8:136, :], own, up, down, 128)
             return 0
 
         lax.fori_loop(0, 6, body, 0)
         for c in range(3):
-            put(BH, c, W[c, 8, 8:136, :], 6 * 128, None, 5 * 128, 128)
-            put(BH, c, W[c, 1, 8:136, :], 7 * 128, 0, None, 128)
-
-    def split_halo(W):
+            put(BH, c, W[c, 8, 8:136, :], BASE[8], None, 5 * 128, 128)
+            put(BH, c, W[c, 1, 8:136, :], BASE[1], 0, None, 128)
+
+    def edge(W, c, xs):
+        return jnp.concatenate([W[c, xs, 0:8, :], W[c, xs, 136:144, :]], 0)
+
+    def split_edges(W):
         for c in range(3):
-            put(BH, c, W[c, 0, 8:136, :], None, 7 * 128, None, 128)
-            put(BH, c, W[c, 9, 8:136, :], None, None, 6 * 128, 128)
-            for xs in range(10):
-                if c == 2 and xs in (0, 9):
-                    continue
-                edge = jnp.concatenate([W[c, xs, 0:8, :], W[c, xs, 136:144, :]], 0)
-                at = (xs - 1) * 16
-                inside = 1 <= xs <= 8
+            for xs in range(1, 9):
+                at = (xs - 2) * 16
                 cross = c < 2
                 put(
-                    BHE, c, edge,
-                    at if inside else None,
-                    at + 16 if xs <= 7 and cross else None,
-                    at - 16 if xs >= 2 and cross else None,
+                    BHE, c, edge(W, c, xs),
+                    at if 2 <= xs <= 7 else None,
+                    at + 16 if xs <= 6 and cross else None,
+                    at - 16 if xs >= 3 and cross else None,
                     16,
                 )
+
+    def split_side(W, xs):
+        base = BASE[xs]
+        for c in range(3):
+            if xs == 1:
+                put(BH, c, W[c, 0, 8:136, :], None, base, None, 128)
+            else:
+                put(BH, c, W[c, 9, 8:136, :], None, None, base, 128)
+            put(BH, c, edge(W, c, xs - 1), None, base + 128, None, 16)
+            put(BH, c, edge(W, c, xs), base + 128, None, None, 16)
+            put(BH, c, edge(W, c, xs + 1), None, None, base + 128, 16)
 
     dot = functools.partial(jnp.dot, preferred_element_type=F32)
 
@@ -265,9 +269,9 @@
         f = dot(BHE[1], wdx)
         g = dot(BHE[1, :, 0:256], wdz)
         for k, a in ((5, e), (6, f), (7, g)):
-            a = a.reshape(8, 16, 128)
-            MU[k, :, 0:8, :] = a[:, 0:8]
-            MU[k, :, 136:144, :] = a[:, 8:16]
+            a = a.reshape(6, 16, 128)
+            MU[k, 1:7, 0:8, :] = a[:, 0:8]
+            MU[k, 1:7, 136:144, :] = a[:, 8:16]
 
     def update(xs, blocks, W, N):
         j = xs - 1
@@ -291,7 +295,7 @@
 
     def substep(p, t, send_after):
         W, N = WS[p], WS[1 - p]
-        split_inner(W)
+        split_own(W)
 
         def body(g, _):
             def store(k, a):
@@ -307,21 +311,15 @@
             return 0
 
         lax.fori_loop(0, 6 // GR, body, 0)
-        finish(p)
-        split_halo(W)
-
-        def store(k, a):
-            MU[k, 7, 8:136, :] = a[0:128]
-            MU[k, 0, 8:136, :] = a[128:256]
-
-        def surf(a):
-            keep_surface(t, 8, a[0:128])
-            keep_surface(t, 1, a[128:256])
-
-        matmuls(6 * 128, 256, store, surf)
+        wait(p, 0, 0)
+        split_edges(W)
         edge_matmuls()
-        update(1, range(16), W, N)
-        update(8, range(16), W, N)
+
+        def body_y(i, _):
+            update(i + 2, (0, 15), W, N)
+            return 0
+
+        lax.fori_loop(0, 6, body_y, 0)
 
         def when_more(f):
             if send_after is True:
@@ -329,17 +327,49 @@
             else:
                 pl.when(send_after)(f)
 
-        when_more(lambda: send_edges_x(1 - p))
-
-        def body_y(i, _):
-            update(i + 2, (0, 15), W, N)
+        def side(xs):
+            out = 1 if xs == 8 else -1
+            wait(p, -out, out)
+            for c in range(3):
+                if xs == 1:
+                    left = PR[p, 0, c]
+                    W[c, 0, 8:72, :] = pltpu.roll(left, 64, 1)
+                    W[c, 0, 72:136, :] = left
+                else:
+                    right = PR[p, 1, c]
+                    W[c, 9, 8:72, :] = right
+                    W[c, 9, 72:136, :] = pltpu.roll(right, 64, 1)
+            split_side(W, xs)
+
+            def store(k, a):
+                MU[k, xs - 1, 8:136, :] = a[0:128]
+                if k >= 5:
+                    MU[k, xs - 1, 0:8, :] = a[128:136]
+                    MU[k, xs - 1, 136:144, :] = a[136:144]
+
+            matmuls(BASE[xs], 144, store, lambda a: keep_surface(t, xs, a[0:128]))
+            update(xs, range(16), W, N)
+            when_more(lambda: send_side(1 - p, xs))
+
+        def both(k, _):
+            is_high = k == jnp.where(gx < GX // 2, 1, 0)
+
+            @pl.when(is_high)
+            def _():
+                side(8)
+
+            @pl.when(jnp.logical_not(is_high))
+            def _():
+                side(1)
+
             return 0
 
-        lax.fori_loop(0, 6, body_y, 0)
-        when_more(lambda: start(1 - p, Y_DIRS))
-
-    send_edges_x(0)
-    start(0, Y_DIRS)
+        lax.fori_loop(0, 2, both, 0)
+        when_more(lambda: start(1 - p, 0))
+
+    send_side(0, 8)
+    send_side(0, 1)
+    start(0, 0)
 
     def pair(i, _):
         substep(0, 2 * i - 1, True)
@@ -511,8 +541,8 @@
             VMEM((3, 10, R, 128), F32),
             VMEM((3, 10, R, 128), F32),
             VMEM((2, 8, 128, 128), F32),
-            VMEM((3, 1024, 512), BF),
-            VMEM((3, 128, 512), BF),
+            VMEM((3, 1056, 512), BF),
+            VMEM((3, 96, 512), BF),
             VMEM((8, 8, R, 128), F32),
             VMEM((8, 128, 128), F32),
             VMEM((2, 2, 3, 64, 128), F32),
@@ -551,7 +581,7 @@
             pltpu.SemaphoreType.DMA((16,)),
             pltpu.SemaphoreType.DMA((2,)),
         ],
-        compiler_params=pltpu.CompilerParams(vmem_limit_bytes=32 * 2**20),
+        compiler_params=pltpu.CompilerParams(vmem_limit_bytes=60 * 2**20),
     )(
         outgoing.reshape(128, 128), support_row, block_col, jnp.transpose(block_val, (0, 2, 3, 1, 4)),
         by_dof(mass_inv), by_dof(bridge_disp), by_dof(bridge_vel), by_dof(bridge_acc), now, before,

time: 106 us -> 191 us (1.80)
  Pallas kernels: 101 us -> 190 us
  local copies, waits for them, and re-layouts: 3.68 us -> 0 us
    pallas_call x1, Pallas kernels: 3.87 us -> 98.1 us  [local(): pl.pallas_call(bridge_kernel, out_shape=[jax.ShapeDtypeStruct((6, 16, 128...]
    pallas_call x1, Pallas kernels: 97.5 us -> 91.6 us  [local(): pl.pallas_call(wave_kernel, out_shape=[jax.ShapeDtypeStruct((3, 1024, 128...]
    unnamed x20 -> x0, local copies, waits for them, and re-layouts: 3.68 us -> none
where the time goes in v3:
time: 191 us; the launch traced here: 190 us
  Pallas kernels  190 us (99%)
    pallas_call x1, Pallas kernels, local(): pl.pallas_call(bridge_kernel, out_shape=[jax.ShapeDtypeStruct((6, 16, 128...  98.1 us
    pallas_call x1, Pallas kernels, local(): pl.pallas_call(wave_kernel, out_shape=[jax.ShapeDtypeStruct((3, 1024, 128...  91.6 us

profile of v3, /device:TPU:1, one launch (start us, length us, event | category | flops | bytes accessed | tf_op | source)
XLA Modules:
  0.0 190.4 jit_solution(4716384539944446027)
XLA Ops:
  0.6 91.6 %shard_map.210 = (f32[3,1024,128]{2,1,0:T(8,128)}, f32[3,1024,128]{2,1,0:T(8,128)}, f32[8,16,128]{2,1,0:T(8,128)}) custom-call(f32[3,1024,128]{2,1,0:T(8,128)} %bitcast.17, f32[3,1024,128]{2,1,0:T(8,128)} %bitcast.18, f32[1024,128]{1,0:T(8,128)} %bitcast.20, f32[1024,128]{1,0:T(8,128)} %bitcast.21, s32[4,128]{1,0:T(4,128)} %bitcast.27, ...), custom_call_target="tpu_custom_call" | custom-call | tf_op jit(solution)/shard_map/pallas_call | solution.py:531
  92.3 98.1 %shard_map.211 = (f32[6,16,128]{2,1,0:T(8,128)}, f32[6,16,128]{2,1,0:T(8,128)}, f32[3,1024,128]{2,1,0:T(8,128)}, f32[3,1024,128]{2,1,0:T(8,128)}) custom-call(f32[128,128]{1,0:T(8,128)} %bitcast.22, s32[2,128]{1,0:T(2,128)} %support.1, s32[16,4,128]{2,1,0:T(4,128)} %col.1, f32[16,6,6,4,128]{4,3,2,1,0:T(4,128)} %bitcast.19, f32[6,16,128]{2,1,0:T(8,128)} %bitcast.23, ...), custom_call_target="tpu_custom_call" | custom-call | tf_op jit(solution)/shard_map/pallas_call | solution.py:572

commit v4 on v3

--- a/solution.py
+++ b/solution.py
@@ -74,8 +74,9 @@
 
 
 def wave_kernel(
-    now, prev, shear, bulk, found, wu, ww, ww0, wv, wv0, wsel, wslot,
+    now_hbm, prev_hbm, shear_hbm, bulk_hbm, found, wu_hbm, ww_hbm, ww0_hbm, wv_hbm, wv0_hbm, wsel_hbm, wslot_hbm,
     out_now, out_prev, out_ground,
+    now, prev, shear, bulk, wu, ww, ww0, wv, wv0, wsel, wslot, in_sem, out_sem,
     WA, WB, SB, BH, BHE, MU, HIST, PS, PR, G1, A1, B1, out_rows,
     send_sem, recv_sem, send_y, recv_y, send_x, recv_x,
 ):
@@ -87,6 +88,16 @@
     dirs = [(1, 0), (-1, 0), (0, 1), (0, -1), (1, 1), (1, -1), (-1, 1), (-1, -1)]
     WS = (WA, WB)
     lane = lax.broadcasted_iota(jnp.int32, (64, 128), 1)
+
+    loads = [pltpu.make_async_copy(now_hbm.at[c], now.at[c], in_sem.at[c]) for c in range(3)]
+    loads += [pltpu.make_async_copy(prev_hbm.at[c], prev.at[c], in_sem.at[3 + c]) for c in range(3)]
+    rest = (
+        (shear_hbm, shear), (bulk_hbm, bulk), (wu_hbm, wu), (ww_hbm, ww), (ww0_hbm, ww0),
+        (wv_hbm, wv), (wv0_hbm, wv0), (wsel_hbm, wsel), (wslot_hbm, wslot),
+    )
+    loads += [pltpu.make_async_copy(src, dst, in_sem.at[6 + i]) for i, (src, dst) in enumerate(rest)]
+    for load in loads:
+        load.start()
 
     for W in WS:
         for xs in (0, 9):
@@ -110,24 +121,21 @@
         def _():
             pl.semaphore_signal(barrier, inc=1, device_id={"gx": gx + dx, "gy": gy + dy}, device_id_type=MESH)
 
+    def turned(read, xs):
+        return jnp.concatenate([read(xs * 4 + xl + 256 * q) for xl in range(4) for q in range(4)], 0).T
+
+    def load_field(src, W, c):
+        def body(i, _):
+            for k in range(4):
+                xs = 4 * i + k
+                W[c, xs + 1, 8:136, :] = turned(lambda at: src[c, pl.ds(at, 8, stride=32), :], xs)
+            return 0
+
+        lax.fori_loop(0, 2, body, 0)
+
     for c in range(3):
-        for src, W in ((now, WA), (prev, WB)):
-
-            def load_field(xs, _):
-                rows = [src[c, pl.ds(xs * 4 + xl + 256 * q, 8, stride=32), :] for xl in range(4) for q in range(4)]
-                W[c, xs + 1, 8:136, :] = jnp.concatenate(rows, 0).T
-                return 0
-
-            lax.fori_loop(0, 8, load_field, 0)
-    for i, src in enumerate((shear, bulk)):
-
-        def load_mod(xs, _):
-            rows = [src[pl.ds(xs * 4 + xl + 256 * q, 8, stride=32), :] for xl in range(4) for q in range(4)]
-            SB[i, xs] = jnp.concatenate(rows, 0).T * (1.0 / 12.0 if i == 0 else 1.0 / 144.0)
-            return 0
-
-        lax.fori_loop(0, 8, load_mod, 0)
-
+        loads[c].wait()
+        load_field(now, WA, c)
     pl.semaphore_wait(barrier, count)
 
     def copy(p, d):
@@ -371,6 +379,23 @@
     send_side(0, 1)
     start(0, 0)
 
+    for c in range(3):
+        loads[3 + c].wait()
+        load_field(prev, WB, c)
+    loads[6].wait()
+    loads[7].wait()
+
+    def load_mod(i, _):
+        for k in range(2):
+            xs = 2 * i + k
+            SB[0, xs] = turned(lambda at: shear[pl.ds(at, 8, stride=32), :], xs) * (1.0 / 12.0)
+            SB[1, xs] = turned(lambda at: bulk[pl.ds(at, 8, stride=32), :], xs) * (1.0 / 144.0)
+        return 0
+
+    lax.fori_loop(0, 4, load_mod, 0)
+    for load in loads[8:]:
+        load.wait()
+
     def pair(i, _):
         substep(0, 2 * i - 1, True)
         substep(1, 2 * i, i < STEPS // 2 - 1)
@@ -388,18 +413,24 @@
 
     lax.fori_loop(0, 8, last, 0)
 
+    stores = [pltpu.make_async_copy(now.at[c], out_now.at[c], out_sem.at[c]) for c in range(3)]
+    stores += [pltpu.make_async_copy(prev.at[c], out_prev.at[c], out_sem.at[3 + c]) for c in range(3)]
+
     def store_fields(which):
-        dst, W = ((out_now, WA), (out_prev, WB))[which]
+        dst, W = ((now, WA), (prev, WB))[which]
         for c in range(3):
 
-            def store_field(xs, _):
-                m = W[c, xs + 1, 8:136, :].T
-                for xl in range(4):
-                    for q in range(4):
-                        dst[c, pl.ds(xs * 4 + xl + 256 * q, 8, stride=32), :] = m[(xl * 4 + q) * 8 : (xl * 4 + q) * 8 + 8]
+            def body(i, _):
+                for k in range(4):
+                    xs = 4 * i + k
+                    m = W[c, xs + 1, 8:136, :].T
+                    for xl in range(4):
+                        for q in range(4):
+                            dst[c, pl.ds(xs * 4 + xl + 256 * q, 8, stride=32), :] = m[(xl * 4 + q) * 8 : (xl * 4 + q) * 8 + 8]
                 return 0
 
-            lax.fori_loop(0, 8, store_field, 0)
+            lax.fori_loop(0, 2, body, 0)
+            stores[3 * which + c].start()
 
     cells = jnp.concatenate([found[...].astype(F32), jnp.zeros((124, 128), F32)], 0).T.astype(jnp.int32)
     rows = jnp.zeros((128, 128), F32)
@@ -448,23 +479,24 @@
     for i in range(1, GX):
         over_x(i).wait()
     out_ground[...] = out_rows[...]
+    for store in stores:
+        store.wait()
 
 
 def bridge_kernel(
     received, support, col, val_hbm, mass, disp, vel, acc, now, before,
     out_disp, out_vel, out_now, out_before,
-    val, ground, state, sem, pass_sem,
+    val, ground, state, held, sem, pass_sem,
 ):
     copies = []
     for node in range(16):
         c = pltpu.make_async_copy(val_hbm.at[node], val.at[:, :, :, node, :], sem.at[node])
         c.start()
         copies.append(c)
-    passed = []
-    for i, (src, dst) in enumerate(((now, out_now), (before, out_before))):
-        c = pltpu.make_async_copy(src, dst, pass_sem.at[i])
+    taken = [pltpu.make_async_copy(src, held.at[i], pass_sem.at[i]) for i, src in enumerate((now, before))]
+    passed = [pltpu.make_async_copy(held.at[i], dst, pass_sem.at[2 + i]) for i, dst in enumerate((out_now, out_before))]
+    for c in taken:
         c.start()
-        passed.append(c)
     rows = jnp.concatenate([support[0:1, :], support[1:2, :]], 1)
     pick = (lax.broadcasted_iota(jnp.int32, (128, 256), 0) == rows // 4).astype(F32).astype(BF)
     flat = received[...].T
@@ -482,6 +514,9 @@
         state[18 + d] = mass[d]
     for c in copies:
         c.wait()
+    for i in range(2):
+        taken[i].wait()
+        passed[i].start()
     sub = lax.broadcasted_iota(jnp.int32, (16, 128), 0)
     index = [col[:, j, :] for j in range(1, 4)]
 
@@ -528,6 +563,7 @@
 ):
     weights = band_weights()
     vm = pl.BlockSpec(memory_space=VMEM)
+    hbm = pl.BlockSpec(memory_space=pl.ANY)
     now, before, outgoing = pl.pallas_call(
         wave_kernel,
         out_shape=[
@@ -535,9 +571,16 @@
             jax.ShapeDtypeStruct((3, 1024, 128), F32),
             jax.ShapeDtypeStruct((GX, GY, 128), F32),
         ],
-        in_specs=[vm] * 12,
-        out_specs=[vm] * 3,
+        in_specs=[hbm] * 4 + [vm] + [hbm] * 7,
+        out_specs=[hbm] * 2 + [vm],
         scratch_shapes=[
+            VMEM((3, 1024, 128), F32),
+            VMEM((3, 1024, 128), F32),
+            VMEM((1024, 128), F32),
+            VMEM((1024, 128), F32),
+            *[VMEM(a.shape, BF) for a in weights],
+            pltpu.SemaphoreType.DMA((15,)),
+            pltpu.SemaphoreType.DMA((6,)),
             VMEM((3, 10, R, 128), F32),
             VMEM((3, 10, R, 128), F32),
             VMEM((2, 8, 128, 128), F32),
@@ -567,7 +610,6 @@
         found_cell.reshape(128, 4).T, *weights,
     )
     by_dof = lambda a: jnp.transpose(a, (1, 0, 2))
-    hbm = pl.BlockSpec(memory_space=pl.ANY)
     field = jax.ShapeDtypeStruct((3, 1024, 128), F32)
     deck_disp, deck_vel, now, before = pl.pallas_call(
         bridge_kernel,
@@ -578,8 +620,9 @@
             VMEM((6, 6, 4, 16, 128), F32),
             VMEM((32, 1, 256), F32),
             VMEM((24, 16, 128), F32),
+            VMEM((2, 3, 1024, 128), F32),
             pltpu.SemaphoreType.DMA((16,)),
-            pltpu.SemaphoreType.DMA((2,)),
+            pltpu.SemaphoreType.DMA((4,)),
         ],
         compiler_params=pltpu.CompilerParams(vmem_limit_bytes=60 * 2**20),
     )(

time: 191 us -> 92 us (0.48)
  Pallas kernels: 190 us -> 91.2 us
    pallas_call x1, Pallas kernels: 98.1 us -> 6.07 us  [local(): pl.pallas_call(bridge_kernel, out_shape=[jax.ShapeDtypeStruct((6, 16, 128...]
    pallas_call x1, Pallas kernels: 91.6 us -> 85.1 us  [local(): pl.pallas_call(wave_kernel, out_shape=[jax.ShapeDtypeStruct((3, 1024, 128...]
where the time goes in v4:
time: 92 us; the launch traced here: 91.8 us
  Pallas kernels  91.2 us (99%)
    pallas_call x1, Pallas kernels, local(): pl.pallas_call(wave_kernel, out_shape=[jax.ShapeDtypeStruct((3, 1024, 128...  85.1 us
    pallas_call x1, Pallas kernels, local(): pl.pallas_call(bridge_kernel, out_shape=[jax.ShapeDtypeStruct((6, 16, 128...  6.07 us

profile of v4, /device:TPU:1, one launch (start us, length us, event | category | flops | bytes accessed | tf_op | source)
XLA Modules:
  0.0 91.8 jit_solution(5119858745394034702)
XLA Ops:
  0.6 85.1 %shard_map.210 = (f32[3,1024,128]{2,1,0:T(8,128)}, f32[3,1024,128]{2,1,0:T(8,128)}, f32[8,16,128]{2,1,0:T(8,128)}) custom-call(f32[3,1024,128]{2,1,0:T(8,128)} %bitcast.17, f32[3,1024,128]{2,1,0:T(8,128)} %bitcast.18, f32[1024,128]{1,0:T(8,128)} %bitcast.20, f32[1024,128]{1,0:T(8,128)} %bitcast.21, s32[4,128]{1,0:T(4,128)} %bitcast.27, ...), custom_call_target="tpu_custom_call" | custom-call | tf_op jit(solution)/shard_map/pallas_call | solution.py:567
  85.7 6.1 %shard_map.211 = (f32[6,16,128]{2,1,0:T(8,128)}, f32[6,16,128]{2,1,0:T(8,128)}, f32[3,1024,128]{2,1,0:T(8,128)}, f32[3,1024,128]{2,1,0:T(8,128)}) custom-call(f32[128,128]{1,0:T(8,128)} %bitcast.22, s32[2,128]{1,0:T(2,128)} %support.1, s32[16,4,128]{2,1,0:T(4,128)} %col.1, f32[16,6,6,4,128]{4,3,2,1,0:T(4,128)} %bitcast.19, f32[6,16,128]{2,1,0:T(8,128)} %bitcast.23, ...), custom_call_target="tpu_custom_call" | custom-call | tf_op jit(solution)/shard_map/pallas_call | solution.py:614

commit v5 on v4

--- a/solution.py
+++ b/solution.py
@@ -85,7 +85,11 @@
     def has(dx, dy):
         return (gx + dx >= 0) & (gx + dx < GX) & (gy + dy >= 0) & (gy + dy < GY)
 
-    dirs = [(1, 0), (-1, 0), (0, 1), (0, -1), (1, 1), (1, -1), (-1, 1), (-1, -1)]
+    dirs = [
+        (1, 1, 8), (1, -1, 8), (0, 1, 8), (0, -1, 8), (1, 0, 8),
+        (-1, 1, 1), (-1, -1, 1), (0, 1, 1), (0, -1, 1), (-1, 0, 1),
+        (0, 1, 0), (0, -1, 0),
+    ]
     WS = (WA, WB)
     lane = lax.broadcasted_iota(jnp.int32, (64, 128), 1)
 
@@ -113,7 +117,7 @@
         pl.semaphore_signal(barrier, inc=1, device_id={"gx": (gx + i) % GX, "gy": gy}, device_id_type=MESH)
     for i in range(1, GY):
         pl.semaphore_signal(barrier, inc=1, device_id={"gx": gx, "gy": (gy + i) % GY}, device_id_type=MESH)
-    for dx, dy in dirs[4:]:
+    for dx, dy in ((1, 1), (1, -1), (-1, 1), (-1, -1)):
         ok = has(dx, dy)
         count = count + ok.astype(jnp.int32)
 
@@ -139,7 +143,7 @@
     pl.semaphore_wait(barrier, count)
 
     def copy(p, d):
-        dx, dy = dirs[d]
+        dx, dy, slab = dirs[d]
         W = WS[p]
         if dy == 0:
             side = 1 if dx > 0 else 0
@@ -147,7 +151,8 @@
         else:
             y_src, y_dst = (134, 6) if dy > 0 else (8, 136)
             if dx == 0:
-                src, dst = W.at[:, 1:9, pl.ds(y_src, 2), :], W.at[:, 1:9, pl.ds(y_dst, 2), :]
+                slabs = pl.ds(slab, 1) if slab else pl.ds(2, 6)
+                src, dst = W.at[:, slabs, pl.ds(y_src, 2), :], W.at[:, slabs, pl.ds(y_dst, 2), :]
             else:
                 x_src, x_dst = (8, 0) if dx > 0 else (1, 9)
                 src, dst = W.at[0:2, x_src, pl.ds(y_src, 2), :], W.at[0:2, x_dst, pl.ds(y_dst, 2), :]
@@ -156,28 +161,27 @@
             device_id={"gx": gx + dx, "gy": gy + dy}, device_id_type=MESH,
         )
 
-    def each(dx, step):
-        for d, (ex, ey) in enumerate(dirs):
-            if ex == dx:
-                pl.when(has(ex, ey) if step != "recv" else has(-ex, -ey))(functools.partial(act, d, step))
-
-    def act(d, step):
-        c = copy(act.p, d)
-        if step == "start":
-            c.start()
-        elif step == "recv":
-            c.wait_recv()
-        else:
-            c.wait_send()
-
-    def start(p, dx):
-        act.p = p
-        each(dx, "start")
+    def start(p, slab):
+        for d, (dx, dy, after) in enumerate(dirs):
+            if after == slab:
+
+                @pl.when(has(dx, dy))
+                def _():
+                    copy(p, d).start()
 
     def wait(p, dx_recv, dx_send):
-        act.p = p
-        each(dx_recv, "recv")
-        each(dx_send, "send")
+        for d, (dx, dy, _) in enumerate(dirs):
+            if dx == dx_recv:
+
+                @pl.when(has(-dx, -dy))
+                def _():
+                    copy(p, d).wait_recv()
+
+            if dx == dx_send:
+
+                @pl.when(has(dx, dy))
+                def _():
+                    copy(p, d).wait_send()
 
     def send_side(p, xs):
         W = WS[p]
@@ -187,7 +191,7 @@
                 PS[p, 1, c] = jnp.where(lane < 64, pltpu.roll(low, 64, 1), high)
             else:
                 PS[p, 0, c] = jnp.where(lane < 64, low, pltpu.roll(high, 64, 1))
-        start(p, 1 if xs == 8 else -1)
+        start(p, xs)
 
     def halves(x):
         hi = x.astype(BF)
@@ -301,6 +305,25 @@
                 b = mix[c] + 12.0 * dyy if c == 1 else mix[c]
                 N[c, xs, r(0), :] = (2.0 * mid - N[c, xs, r(0), :]) + (sh * lap + bu * b)
 
+    stores = [pltpu.make_async_copy(now.at[c], out_now.at[c], out_sem.at[c]) for c in range(3)]
+    stores += [pltpu.make_async_copy(prev.at[c], out_prev.at[c], out_sem.at[3 + c]) for c in range(3)]
+
+    def store_fields(which, components):
+        dst, W = ((now, WA), (prev, WB))[which]
+        for c in components:
+
+            def body(i, _):
+                for k in range(4):
+                    xs = 4 * i + k
+                    m = W[c, xs + 1, 8:136, :].T
+                    for xl in range(4):
+                        for q in range(4):
+                            dst[c, pl.ds(xs * 4 + xl + 256 * q, 8, stride=32), :] = m[(xl * 4 + q) * 8 : (xl * 4 + q) * 8 + 8]
+                return 0
+
+            lax.fori_loop(0, 2, body, 0)
+            stores[3 * which + c].start()
+
     def substep(p, t, send_after):
         W, N = WS[p], WS[1 - p]
         split_own(W)
@@ -334,6 +357,8 @@
                 f()
             else:
                 pl.when(send_after)(f)
+
+        when_more(lambda: start(1 - p, 0))
 
         def side(xs):
             out = 1 if xs == 8 else -1
@@ -372,8 +397,13 @@
 
             return 0
 
+        if p == 1:
+
+            @pl.when(jnp.logical_not(send_after))
+            def _():
+                store_fields(1, range(3))
+
         lax.fori_loop(0, 2, both, 0)
-        when_more(lambda: start(1 - p, 0))
 
     send_side(0, 8)
     send_side(0, 1)
@@ -412,25 +442,6 @@
         return 0
 
     lax.fori_loop(0, 8, last, 0)
-
-    stores = [pltpu.make_async_copy(now.at[c], out_now.at[c], out_sem.at[c]) for c in range(3)]
-    stores += [pltpu.make_async_copy(prev.at[c], out_prev.at[c], out_sem.at[3 + c]) for c in range(3)]
-
-    def store_fields(which):
-        dst, W = ((now, WA), (prev, WB))[which]
-        for c in range(3):
-
-            def body(i, _):
-                for k in range(4):
-                    xs = 4 * i + k
-                    m = W[c, xs + 1, 8:136, :].T
-                    for xl in range(4):
-                        for q in range(4):
-                            dst[c, pl.ds(xs * 4 + xl + 256 * q, 8, stride=32), :] = m[(xl * 4 + q) * 8 : (xl * 4 + q) * 8 + 8]
-                return 0
-
-            lax.fori_loop(0, 2, body, 0)
-            stores[3 * which + c].start()
 
     cells = jnp.concatenate([found[...].astype(F32), jnp.zeros((124, 128), F32)], 0).T.astype(jnp.int32)
     rows = jnp.zeros((128, 128), F32)
@@ -467,7 +478,7 @@
     for i in range(1, GY):
         over_y(i).start()
     A1[gy] = G1[gy]
-    store_fields(0)
+    store_fields(0, range(2))
     for i in range(1, GY):
         over_y(i).wait()
     for i in range(GX):
@@ -475,7 +486,7 @@
     for i in range(1, GX):
         over_x(i).start()
     out_rows[gx] = B1[gx]
-    store_fields(1)
+    store_fields(0, range(2, 3))
     for i in range(1, GX):
         over_x(i).wait()
     out_ground[...] = out_rows[...]
@@ -495,8 +506,6 @@
         copies.append(c)
     taken = [pltpu.make_async_copy(src, held.at[i], pass_sem.at[i]) for i, src in enumerate((now, before))]
     passed = [pltpu.make_async_copy(held.at[i], dst, pass_sem.at[2 + i]) for i, dst in enumerate((out_now, out_before))]
-    for c in taken:
-        c.start()
     rows = jnp.concatenate([support[0:1, :], support[1:2, :]], 1)
     pick = (lax.broadcasted_iota(jnp.int32, (128, 256), 0) == rows // 4).astype(F32).astype(BF)
     flat = received[...].T
@@ -514,9 +523,8 @@
         state[18 + d] = mass[d]
     for c in copies:
         c.wait()
-    for i in range(2):
-        taken[i].wait()
-        passed[i].start()
+    for c in taken:
+        c.start()
     sub = lax.broadcasted_iota(jnp.int32, (16, 128), 0)
     index = [col[:, j, :] for j in range(1, 4)]
 
@@ -549,7 +557,11 @@
             state[D + d] = new[d]
         return 0
 
-    lax.fori_loop(0, STEPS, step, 0)
+    lax.fori_loop(0, STEPS // 2, step, 0)
+    for i in range(2):
+        taken[i].wait()
+        passed[i].start()
+    lax.fori_loop(STEPS // 2, STEPS, step, 0)
     for d in range(6):
         out_disp[d] = state[D + d]
         out_vel[d] = state[V + d]
@@ -594,8 +606,8 @@
             VMEM((GY, GX, 128), F32),
             VMEM((GX, GY, 128), F32),
             VMEM((GX, GY, 128), F32),
-            pltpu.SemaphoreType.DMA((2, 8)),
-            pltpu.SemaphoreType.DMA((2, 8)),
+            pltpu.SemaphoreType.DMA((2, 12)),
+            pltpu.SemaphoreType.DMA((2, 12)),
             pltpu.SemaphoreType.DMA((GY,)),
             pltpu.SemaphoreType.DMA((GY,)),
             pltpu.SemaphoreType.DMA((GX,)),
@@ -624,7 +636,7 @@
             pltpu.SemaphoreType.DMA((16,)),
             pltpu.SemaphoreType.DMA((4,)),
         ],
-        compiler_params=pltpu.CompilerParams(vmem_limit_bytes=60 * 2**20),
+        compiler_params=pltpu.CompilerParams(vmem_limit_bytes=52 * 2**20),
     )(
         outgoing.reshape(128, 128), support_row, block_col, jnp.transpose(block_val, (0, 2, 3, 1, 4)),
         by_dof(mass_inv), by_dof(bridge_disp), by_dof(bridge_vel), by_dof(bridge_acc), now, before,

time: 92 us -> 88.7 us (0.964)
  Pallas kernels: 91.2 us -> 86.9 us
    pallas_call x1, Pallas kernels: 85.1 us -> 81.9 us  [local(): pl.pallas_call(wave_kernel, out_shape=[jax.ShapeDtypeStruct((3, 1024, 128...]
    pallas_call x1, Pallas kernels: 6.07 us -> 5.02 us  [local(): pl.pallas_call(bridge_kernel, out_shape=[jax.ShapeDtypeStruct((6, 16, 128...]
where the time goes in v5:
time: 88.7 us; the launch traced here: 88.5 us
  Pallas kernels  86.9 us (98%)
    pallas_call x1, Pallas kernels, local(): pl.pallas_call(wave_kernel, out_shape=[jax.ShapeDtypeStruct((3, 1024, 128...  81.9 us
    pallas_call x1, Pallas kernels, local(): pl.pallas_call(bridge_kernel, out_shape=[jax.ShapeDtypeStruct((6, 16, 128...  5.02 us

profile of v5, /device:TPU:1, one launch (start us, length us, event | category | flops | bytes accessed | tf_op | source)
XLA Modules:
  0.0 88.5 jit_solution(1694821900420855336)
XLA Ops:
  0.6 0.0 copy-start
  0.6 0.0 copy-start.2
  0.7 0.0 copy-start.3
  0.7 0.0 copy-start.4
  0.7 0.0 copy-start.5
  0.7 0.0 copy-start.6
  0.7 0.0 copy-start.7
  0.7 81.9 %shard_map.210 = (f32[3,1024,128]{2,1,0:T(8,128)}, f32[3,1024,128]{2,1,0:T(8,128)}, f32[8,16,128]{2,1,0:T(8,128)}) custom-call(f32[3,1024,128]{2,1,0:T(8,128)} %bitcast.23, f32[3,1024,128]{2,1,0:T(8,128)} %bitcast.24, f32[1024,128]{1,0:T(8,128)} %bitcast.25, f32[1024,128]{1,0:T(8,128)} %bitcast.26, s32[4,128]{1,0:T(4,128)} %bitcast.27, ...), custom_call_target="tpu_custom_call" | custom-call | tf_op jit(solution)/shard_map/pallas_call | solution.py:579
  82.6 0.0 copy-done
  82.6 0.0 copy-done.2
  82.6 0.0 copy-done.3
  82.6 0.0 copy-done.4
  82.6 0.0 copy-done.5
  82.6 0.0 copy-done.6
  82.6 0.0 copy-done.7
  82.6 0.0 copy-start.1
  82.6 0.8 copy-done.1
  83.5 5.0 %shard_map.211 = (f32[6,16,128]{2,1,0:T(8,128)}, f32[6,16,128]{2,1,0:T(8,128)}, f32[3,1024,128]{2,1,0:T(8,128)}, f32[3,1024,128]{2,1,0:T(8,128)}) custom-call(f32[128,128]{1,0:T(8,128)S(1)} %bitcast.18, s32[2,128]{1,0:T(2,128)S(1)} %copy-done.7, s32[16,4,128]{2,1,0:T(4,128)S(1)} %copy-done.6, f32[16,6,6,4,128]{4,3,2,1,0:T(4,128)S(1)} %bitcast.17, ...), custom_call_target="tpu_custom_call" | custom-call | tf_op jit(solution)/shard_map/pallas_call | solution.py:626
Async XLA Ops:
  0.6 81.9 %copy-start = (f32[16,4,6,6,128]{4,1,3,2,0:T(4,128)S(1)}, f32[16,4,6,6,128]{4,1,3,2,0:T(4,128)}, u32[]{:S(2)}) copy-start(f32[16,4,6,6,128]{4,1,3,2,0:T(4,128)} %param.26) | copy-start | bytes 3538948
  0.6 81.9 %copy-start.2 = (f32[16,6,128]{2,0,1:T(8,128)S(1)}, f32[16,6,128]{2,0,1:T(8,128)}, u32[]{:S(2)}) copy-start(f32[16,6,128]{2,0,1:T(8,128)} %param.27) | copy-start | bytes 147460
  0.7 81.9 %copy-start.3 = (f32[16,6,128]{2,0,1:T(8,128)S(1)}, f32[16,6,128]{2,0,1:T(8,128)}, u32[]{:S(2)}) copy-start(f32[16,6,128]{2,0,1:T(8,128)} %param.28) | copy-start | bytes 147460
  0.7 81.9 %copy-start.4 = (f32[16,6,128]{2,0,1:T(8,128)S(1)}, f32[16,6,128]{2,0,1:T(8,128)}, u32[]{:S(2)}) copy-start(f32[16,6,128]{2,0,1:T(8,128)} %param.29) | copy-start | bytes 147460
  0.7 81.9 %copy-start.5 = (f32[16,6,128]{2,0,1:T(8,128)S(1)}, f32[16,6,128]{2,0,1:T(8,128)}, u32[]{:S(2)}) copy-start(f32[16,6,128]{2,0,1:T(8,128)} %param.30) | copy-start | bytes 147460
  0.7 81.9 %copy-start.6 = (s32[16,4,128]{2,1,0:T(4,128)S(1)}, s32[16,4,128]{2,1,0:T(4,128)}, u32[]{:S(2)}) copy-start(s32[16,4,128]{2,1,0:T(4,128)} %col.1) | copy-start | bytes 98308
  0.7 81.9 %copy-start.7 = (s32[2,128]{1,0:T(2,128)S(1)}, s32[2,128]{1,0:T(2,128)}, u32[]{:S(2)}) copy-start(s32[2,128]{1,0:T(2,128)} %support.1) | copy-start | bytes 3076
  82.6 0.8 copy-start.1

commit v6 on v5

--- a/solution.py
+++ b/solution.py
@@ -385,7 +385,7 @@
             when_more(lambda: send_side(1 - p, xs))
 
         def both(k, _):
-            is_high = k == jnp.where(gx < GX // 2, 1, 0)
+            is_high = k == gx % 2
 
             @pl.when(is_high)
             def _():
@@ -495,10 +495,12 @@
 
 
 def bridge_kernel(
-    received, support, col, val_hbm, mass, disp, vel, acc, now, before,
+    received_hbm, support, col, val_hbm, mass, disp, vel, acc, now, before,
     out_disp, out_vel, out_now, out_before,
-    val, ground, state, held, sem, pass_sem,
+    val, ground, state, held, received, sem, pass_sem,
 ):
+    arrive = pltpu.make_async_copy(received_hbm, received, pass_sem.at[4])
+    arrive.start()
     copies = []
     for node in range(16):
         c = pltpu.make_async_copy(val_hbm.at[node], val.at[:, :, :, node, :], sem.at[node])
@@ -508,6 +510,7 @@
     passed = [pltpu.make_async_copy(held.at[i], dst, pass_sem.at[2 + i]) for i, dst in enumerate((out_now, out_before))]
     rows = jnp.concatenate([support[0:1, :], support[1:2, :]], 1)
     pick = (lax.broadcasted_iota(jnp.int32, (128, 256), 0) == rows // 4).astype(F32).astype(BF)
+    arrive.wait()
     flat = received[...].T
     hi = flat.astype(BF)
     lo = (flat - hi.astype(F32)).astype(BF)
@@ -626,15 +629,16 @@
     deck_disp, deck_vel, now, before = pl.pallas_call(
         bridge_kernel,
         out_shape=[jax.ShapeDtypeStruct((6, 16, 128), F32)] * 2 + [field] * 2,
-        in_specs=[vm] * 3 + [hbm] + [vm] * 4 + [hbm] * 2,
+        in_specs=[hbm] + [vm] * 2 + [hbm] + [vm] * 4 + [hbm] * 2,
         out_specs=[vm] * 2 + [hbm] * 2,
         scratch_shapes=[
             VMEM((6, 6, 4, 16, 128), F32),
             VMEM((32, 1, 256), F32),
             VMEM((24, 16, 128), F32),
             VMEM((2, 3, 1024, 128), F32),
+            VMEM((128, 128), F32),
             pltpu.SemaphoreType.DMA((16,)),
-            pltpu.SemaphoreType.DMA((4,)),
+            pltpu.SemaphoreType.DMA((5,)),
         ],
         compiler_params=pltpu.CompilerParams(vmem_limit_bytes=52 * 2**20),
     )(

time: 88.7 us -> 89.1 us (level)
  no operation moved by 1% of the time
where the time goes in v6:
time: 89.1 us; the launch traced here: 88.9 us
  Pallas kernels  87.3 us (98%)
    pallas_call x1, Pallas kernels, local(): pl.pallas_call(wave_kernel, out_shape=[jax.ShapeDtypeStruct((3, 1024, 128...  82.2 us
    pallas_call x1, Pallas kernels, local(): pl.pallas_call(bridge_kernel, out_shape=[jax.ShapeDtypeStruct((6, 16, 128...  5.11 us

profile of v6, /device:TPU:1, one launch (start us, length us, event | category | flops | bytes accessed | tf_op | source)
XLA Modules:
  0.0 88.9 jit_solution(8075107736280259269)
XLA Ops:
  0.6 0.0 copy-start
  0.6 0.0 copy-start.2
  0.7 0.0 copy-start.3
  0.7 0.0 copy-start.4
  0.7 0.0 copy-start.5
  0.7 0.0 copy-start.6
  0.7 0.0 copy-start.7
  0.7 82.2 %shard_map.210 = (f32[3,1024,128]{2,1,0:T(8,128)}, f32[3,1024,128]{2,1,0:T(8,128)}, f32[8,16,128]{2,1,0:T(8,128)}) custom-call(f32[3,1024,128]{2,1,0:T(8,128)} %bitcast.23, f32[3,1024,128]{2,1,0:T(8,128)} %bitcast.24, f32[1024,128]{1,0:T(8,128)} %bitcast.25, f32[1024,128]{1,0:T(8,128)} %bitcast.26, s32[4,128]{1,0:T(4,128)} %bitcast.27, ...), custom_call_target="tpu_custom_call" | custom-call | tf_op jit(solution)/shard_map/pallas_call | solution.py:582
  82.9 0.0 copy-done
  82.9 0.0 copy-done.2
  82.9 0.0 copy-done.3
  82.9 0.0 copy-done.4
  82.9 0.0 copy-done.5
  82.9 0.0 copy-done.6
  83.0 0.0 copy-done.7
  83.0 0.0 copy-start.1
  83.0 0.8 copy-done.1
  83.8 5.1 %shard_map.211 = (f32[6,16,128]{2,1,0:T(8,128)}, f32[6,16,128]{2,1,0:T(8,128)}, f32[3,1024,128]{2,1,0:T(8,128)}, f32[3,1024,128]{2,1,0:T(8,128)}) custom-call(f32[128,128]{1,0:T(8,128)S(1)} %bitcast.18, s32[2,128]{1,0:T(2,128)S(1)} %copy-done.7, s32[16,4,128]{2,1,0:T(4,128)S(1)} %copy-done.6, f32[16,6,6,4,128]{4,3,2,1,0:T(4,128)S(1)} %bitcast.17, ...), custom_call_target="tpu_custom_call" | custom-call | tf_op jit(solution)/shard_map/pallas_call | solution.py:629
Async XLA Ops:
  0.6 82.3 %copy-start = (f32[16,4,6,6,128]{4,1,3,2,0:T(4,128)S(1)}, f32[16,4,6,6,128]{4,1,3,2,0:T(4,128)}, u32[]{:S(2)}) copy-start(f32[16,4,6,6,128]{4,1,3,2,0:T(4,128)} %param.26) | copy-start | bytes 3538948
  0.6 82.3 %copy-start.2 = (f32[16,6,128]{2,0,1:T(8,128)S(1)}, f32[16,6,128]{2,0,1:T(8,128)}, u32[]{:S(2)}) copy-start(f32[16,6,128]{2,0,1:T(8,128)} %param.27) | copy-start | bytes 147460
  0.7 82.3 %copy-start.3 = (f32[16,6,128]{2,0,1:T(8,128)S(1)}, f32[16,6,128]{2,0,1:T(8,128)}, u32[]{:S(2)}) copy-start(f32[16,6,128]{2,0,1:T(8,128)} %param.28) | copy-start | bytes 147460
  0.7 82.3 %copy-start.4 = (f32[16,6,128]{2,0,1:T(8,128)S(1)}, f32[16,6,128]{2,0,1:T(8,128)}, u32[]{:S(2)}) copy-start(f32[16,6,128]{2,0,1:T(8,128)} %param.29) | copy-start | bytes 147460
  0.7 82.3 %copy-start.5 = (f32[16,6,128]{2,0,1:T(8,128)S(1)}, f32[16,6,128]{2,0,1:T(8,128)}, u32[]{:S(2)}) copy-start(f32[16,6,128]{2,0,1:T(8,128)} %param.30) | copy-start | bytes 147460
  0.7 82.3 %copy-start.6 = (s32[16,4,128]{2,1,0:T(4,128)S(1)}, s32[16,4,128]{2,1,0:T(4,128)}, u32[]{:S(2)}) copy-start(s32[16,4,128]{2,1,0:T(4,128)} %col.1) | copy-start | bytes 98308
  0.7 82.3 %copy-start.7 = (s32[2,128]{1,0:T(2,128)S(1)}, s32[2,128]{1,0:T(2,128)}, u32[]{:S(2)}) copy-start(s32[2,128]{1,0:T(2,128)} %support.1) | copy-start | bytes 3076
  83.0 0.8 copy-start.1

commit v7 on v5

--- a/solution.py
+++ b/solution.py
@@ -241,16 +241,28 @@
                     16,
                 )
 
-    def split_side(W, xs):
+    def split_side_own(W, xs):
+        base = BASE[xs] + 128
+        for c in range(3):
+            put(BH, c, edge(W, c, xs), base, None, None, 16)
+            if xs == 1:
+                put(BH, c, edge(W, c, 2), None, None, base, 16)
+            else:
+                put(BH, c, edge(W, c, 7), None, base, None, 16)
+
+    def split_side_halo(W, p, xs):
         base = BASE[xs]
         for c in range(3):
             if xs == 1:
-                put(BH, c, W[c, 0, 8:136, :], None, base, None, 128)
+                left = PR[p, 0, c]
+                put(BH, c, pltpu.roll(left, 64, 1), None, base, None, 64)
+                put(BH, c, left, None, base + 64, None, 64)
+                put(BH, c, edge(W, c, 0), None, base + 128, None, 16)
             else:
-                put(BH, c, W[c, 9, 8:136, :], None, None, base, 128)
-            put(BH, c, edge(W, c, xs - 1), None, base + 128, None, 16)
-            put(BH, c, edge(W, c, xs), base + 128, None, None, 16)
-            put(BH, c, edge(W, c, xs + 1), None, None, base + 128, 16)
+                right = PR[p, 1, c]
+                put(BH, c, right, None, None, base, 64)
+                put(BH, c, pltpu.roll(right, 64, 1), None, None, base + 64, 64)
+                put(BH, c, edge(W, c, 9), None, None, base + 128, 16)
 
     dot = functools.partial(jnp.dot, preferred_element_type=F32)
 
@@ -362,17 +374,9 @@
 
         def side(xs):
             out = 1 if xs == 8 else -1
+            split_side_own(W, xs)
             wait(p, -out, out)
-            for c in range(3):
-                if xs == 1:
-                    left = PR[p, 0, c]
-                    W[c, 0, 8:72, :] = pltpu.roll(left, 64, 1)
-                    W[c, 0, 72:136, :] = left
-                else:
-                    right = PR[p, 1, c]
-                    W[c, 9, 8:72, :] = right
-                    W[c, 9, 72:136, :] = pltpu.roll(right, 64, 1)
-            split_side(W, xs)
+            split_side_halo(W, p, xs)
 
             def store(k, a):
                 MU[k, xs - 1, 8:136, :] = a[0:128]

time: 88.7 us -> 88.7 us (level)
  no operation moved by 1% of the time
where the time goes in v7:
time: 88.7 us; the launch traced here: 88.5 us
  Pallas kernels  86.9 us (98%)
    pallas_call x1, Pallas kernels, local(): pl.pallas_call(wave_kernel, out_shape=[jax.ShapeDtypeStruct((3, 1024, 128...  81.9 us
    pallas_call x1, Pallas kernels, local(): pl.pallas_call(bridge_kernel, out_shape=[jax.ShapeDtypeStruct((6, 16, 128...  5.02 us

profile of v7, /device:TPU:1, one launch (start us, length us, event | category | flops | bytes accessed | tf_op | source)
XLA Modules:
  0.0 88.5 jit_solution(9584226624819504901)
XLA Ops:
  0.6 0.0 copy-start
  0.6 0.0 copy-start.2
  0.7 0.0 copy-start.3
  0.7 0.0 copy-start.4
  0.7 0.0 copy-start.5
  0.7 0.0 copy-start.6
  0.7 0.0 copy-start.7
  0.7 81.9 %shard_map.210 = (f32[3,1024,128]{2,1,0:T(8,128)}, f32[3,1024,128]{2,1,0:T(8,128)}, f32[8,16,128]{2,1,0:T(8,128)}) custom-call(f32[3,1024,128]{2,1,0:T(8,128)} %bitcast.23, f32[3,1024,128]{2,1,0:T(8,128)} %bitcast.24, f32[1024,128]{1,0:T(8,128)} %bitcast.25, f32[1024,128]{1,0:T(8,128)} %bitcast.26, s32[4,128]{1,0:T(4,128)} %bitcast.27, ...), custom_call_target="tpu_custom_call" | custom-call | tf_op jit(solution)/shard_map/pallas_call | solution.py:583
  82.6 0.0 copy-done
  82.6 0.0 copy-done.2
  82.6 0.0 copy-done.3
  82.6 0.0 copy-done.4
  82.6 0.0 copy-done.5
  82.6 0.0 copy-done.6
  82.6 0.0 copy-done.7
  82.6 0.0 copy-start.1
  82.7 0.8 copy-done.1
  83.5 5.0 %shard_map.211 = (f32[6,16,128]{2,1,0:T(8,128)}, f32[6,16,128]{2,1,0:T(8,128)}, f32[3,1024,128]{2,1,0:T(8,128)}, f32[3,1024,128]{2,1,0:T(8,128)}) custom-call(f32[128,128]{1,0:T(8,128)S(1)} %bitcast.18, s32[2,128]{1,0:T(2,128)S(1)} %copy-done.7, s32[16,4,128]{2,1,0:T(4,128)S(1)} %copy-done.6, f32[16,6,6,4,128]{4,3,2,1,0:T(4,128)S(1)} %bitcast.17, ...), custom_call_target="tpu_custom_call" | custom-call | tf_op jit(solution)/shard_map/pallas_call | solution.py:630
Async XLA Ops:
  0.6 81.9 %copy-start = (f32[16,4,6,6,128]{4,1,3,2,0:T(4,128)S(1)}, f32[16,4,6,6,128]{4,1,3,2,0:T(4,128)}, u32[]{:S(2)}) copy-start(f32[16,4,6,6,128]{4,1,3,2,0:T(4,128)} %param.26) | copy-start | bytes 3538948
  0.6 81.9 %copy-start.2 = (f32[16,6,128]{2,0,1:T(8,128)S(1)}, f32[16,6,128]{2,0,1:T(8,128)}, u32[]{:S(2)}) copy-start(f32[16,6,128]{2,0,1:T(8,128)} %param.27) | copy-start | bytes 147460
  0.7 81.9 %copy-start.3 = (f32[16,6,128]{2,0,1:T(8,128)S(1)}, f32[16,6,128]{2,0,1:T(8,128)}, u32[]{:S(2)}) copy-start(f32[16,6,128]{2,0,1:T(8,128)} %param.28) | copy-start | bytes 147460
  0.7 81.9 %copy-start.4 = (f32[16,6,128]{2,0,1:T(8,128)S(1)}, f32[16,6,128]{2,0,1:T(8,128)}, u32[]{:S(2)}) copy-start(f32[16,6,128]{2,0,1:T(8,128)} %param.29) | copy-start | bytes 147460
  0.7 81.9 %copy-start.5 = (f32[16,6,128]{2,0,1:T(8,128)S(1)}, f32[16,6,128]{2,0,1:T(8,128)}, u32[]{:S(2)}) copy-start(f32[16,6,128]{2,0,1:T(8,128)} %param.30) | copy-start | bytes 147460
  0.7 81.9 %copy-start.6 = (s32[16,4,128]{2,1,0:T(4,128)S(1)}, s32[16,4,128]{2,1,0:T(4,128)}, u32[]{:S(2)}) copy-start(s32[16,4,128]{2,1,0:T(4,128)} %col.1) | copy-start | bytes 98308
  0.7 81.9 %copy-start.7 = (s32[2,128]{1,0:T(2,128)S(1)}, s32[2,128]{1,0:T(2,128)}, u32[]{:S(2)}) copy-start(s32[2,128]{1,0:T(2,128)} %support.1) | copy-start | bytes 3076
  82.6 0.8 copy-start.1
